TPU v7x, 32 devices: a whole 2x2x4 slice. The times are simulated.
32 devices in a mesh: dp: 4 (over x, core), fsdp: 8 (over z, y).
Axes of the slice: x: 2, y: 2, z: 4, core: 2. Of those that a mesh axis runs over, the one named last changes fastest.
Arguments:
- block_input: bfloat16 [32, 512, 576], P(('dp', 'fsdp')), may hold values from -18 to 18
- lengths: int32 [32], P(('dp', 'fsdp')), may hold values from 128 to 512, as said below
- attention_gain: float32 [576], replicated, may hold values from 0.1 to 1.9
- query_weight: bfloat16 [576, 576], P('dp', 'fsdp'), may hold values from -0.25 to 0.25
- key_matrix: bfloat16 [576, 192], P('dp', 'fsdp'), may hold values from -0.25 to 0.25
- value_matrix: bfloat16 [576, 192], P('dp', 'fsdp'), may hold values from -0.25 to 0.25
- output_weight: bfloat16 [576, 576], P('dp', 'fsdp'), may hold values from -1 to 1
- mlp_gain: float32 [576], replicated, may hold values from 0.1 to 1.9
- gate_weight: bfloat16 [576, 1536], P('dp', 'fsdp'), may hold values from -0.25 to 0.25
- up_weight: bfloat16 [576, 1536], P('dp', 'fsdp'), may hold values from -0.25 to 0.25
- down_weight: bfloat16 [1536, 576], P('dp', 'fsdp'), may hold values from -0.15625 to 0.15625
- cotangent: bfloat16 [32, 512, 576], P(('dp', 'fsdp')), may hold values from -6 to 6
Outputs:
- block_output: bfloat16 [32, 512, 576], P(('dp', 'fsdp'))
- input_grad: float32 [32, 512, 576], P(('dp', 'fsdp'))
- grad_attention_gain: float32 [576], replicated
- grad_query: float32 [576, 576], P('dp', 'fsdp')
- grad_key: float32 [576, 192], P('dp', 'fsdp')
- grad_value: float32 [576, 192], P('dp', 'fsdp')
- grad_output: float32 [576, 576], P('dp', 'fsdp')
- grad_mlp_gain: float32 [576], replicated
- grad_gate: float32 [576, 1536], P('dp', 'fsdp')
- grad_up: float32 [576, 1536], P('dp', 'fsdp')
- grad_down: float32 [1536, 576], P('dp', 'fsdp')
- stream_rms: float32 [2, 3], replicated
Inputs may be any that keep to these rules, and one draw needn't show every extreme that they name: `lengths`: slots are filled from their first place; some slot has exactly 512 valid tokens and some slot exactly 128.
All inputs are finite; a program needn't handle non-finite values.
Results may differ from a plain program's by a relative error of at most 0.022.
Values may be sent and summed in bfloat16 or wider, within the bound.
A program may use at most 192 MiB of HBM per device.

v0:
```python
import jax
import jax.numpy as jnp
from jax import lax
from jax.sharding import PartitionSpec as P

MODEL_WIDTH = 576
QUERY_HEADS = 9
KEY_VALUE_HEADS = 3
HEAD_SIZE = 64
SLOT_PLACES = 512


ROPE_BASE = 10000.0
NORM_EPS = 1e-05


def rms_scale(stream, gain_vector):
    return (
        stream
        * lax.rsqrt(jnp.mean(stream * stream, axis=-1, keepdims=True) + NORM_EPS)
        * gain_vector
    )


def apply_rotation(value_rows, head_count, direction):
    place_count = value_rows.shape[-2]
    half_width = HEAD_SIZE // 2
    inverse = ROPE_BASE ** (-(2.0 * jnp.arange(half_width, dtype=jnp.float32)) / HEAD_SIZE)
    angles = jnp.arange(place_count, dtype=jnp.float32)[:, None] * inverse[None, :]
    cos_table = jnp.cos(angles)[:, None, :]
    sin_table = direction * jnp.sin(angles)[:, None, :]
    shaped = value_rows.reshape(value_rows.shape[:-1] + (head_count, HEAD_SIZE))
    first_half = shaped[..., :half_width]
    second_half = shaped[..., half_width:]
    turned = jnp.concatenate(
        [
            first_half * cos_table - second_half * sin_table,
            second_half * cos_table + first_half * sin_table,
        ],
        axis=-1,
    )
    return turned.reshape(value_rows.shape)


def key_mask(first_row, stop_row, length):
    query_places = first_row + jnp.arange(stop_row - first_row, dtype=jnp.int32)
    key_places = jnp.arange(stop_row, dtype=jnp.int32)
    return (key_places[None, :] <= query_places[:, None]) & (key_places[None, :] < length)


def attend_forward(packed):
    query_rows, rotated_keys, value_rows, length = packed
    group_total = QUERY_HEADS // KEY_VALUE_HEADS
    rows_per_step = min(512, SLOT_PLACES)
    scale_factor = HEAD_SIZE ** (-0.5)
    heads_of_query = query_rows[0:rows_per_step].reshape(
        rows_per_step, KEY_VALUE_HEADS, group_total, HEAD_SIZE
    )
    heads_of_key = rotated_keys[:rows_per_step].reshape(rows_per_step, KEY_VALUE_HEADS, HEAD_SIZE)
    heads_of_value = value_rows[:rows_per_step].reshape(rows_per_step, KEY_VALUE_HEADS, HEAD_SIZE)
    scores = jnp.einsum(
        "qngd,knd->ngqk", heads_of_query, heads_of_key, preferred_element_type=jnp.float32
    )
    allowed = key_mask(0, rows_per_step, length)
    logits = jnp.where(allowed, scores * scale_factor, -1e30)
    highest = jnp.max(logits, axis=-1, keepdims=True)
    expo_terms = jnp.exp(logits - highest)
    total = jnp.sum(expo_terms, axis=-1, keepdims=True)
    chances = (expo_terms / total).astype(jnp.bfloat16)
    mixed_heads = jnp.einsum(
        "ngqk,knd->qngd", chances, heads_of_value, preferred_element_type=jnp.float32
    )
    outputs = [mixed_heads.reshape(rows_per_step, QUERY_HEADS * HEAD_SIZE)]
    log_sums = [highest + jnp.log(total)]
    return (jnp.concatenate(outputs, axis=0), jnp.concatenate(log_sums, axis=2))


def attend_backward(packed):
    query_rows, rotated_keys, value_rows, output_gradient, log_sums, length = packed
    group_total = QUERY_HEADS // KEY_VALUE_HEADS
    rows_per_step = min(512, SLOT_PLACES)
    scale_factor = HEAD_SIZE ** (-0.5)
    key_gradient = jnp.zeros((SLOT_PLACES, KEY_VALUE_HEADS, HEAD_SIZE), jnp.float32)
    value_gradient = jnp.zeros((SLOT_PLACES, KEY_VALUE_HEADS, HEAD_SIZE), jnp.float32)
    heads_of_query = query_rows[0:rows_per_step].reshape(
        rows_per_step, KEY_VALUE_HEADS, group_total, HEAD_SIZE
    )
    head_gradient = output_gradient[0:rows_per_step].reshape(
        rows_per_step, KEY_VALUE_HEADS, group_total, HEAD_SIZE
    )
    heads_of_key = rotated_keys[:rows_per_step].reshape(rows_per_step, KEY_VALUE_HEADS, HEAD_SIZE)
    heads_of_value = value_rows[:rows_per_step].reshape(rows_per_step, KEY_VALUE_HEADS, HEAD_SIZE)
    scores = jnp.einsum(
        "qngd,knd->ngqk", heads_of_query, heads_of_key, preferred_element_type=jnp.float32
    )
    allowed = key_mask(0, rows_per_step, length)
    logits = jnp.where(allowed, scores * scale_factor, -1e30)
    chances = jnp.exp(logits - log_sums[:, :, 0:rows_per_step])
    grad_chances = jnp.einsum(
        "qngd,knd->ngqk", head_gradient, heads_of_value, preferred_element_type=jnp.float32
    )
    inner = jnp.sum(chances * grad_chances, axis=-1, keepdims=True)
    grad_scores = jnp.where(allowed, chances * (grad_chances - inner) * scale_factor, 0.0).astype(
        jnp.bfloat16
    )
    query_grad = jnp.einsum(
        "ngqk,knd->qngd", grad_scores, heads_of_key, preferred_element_type=jnp.float32
    )
    query_parts = [query_grad.reshape(rows_per_step, QUERY_HEADS * HEAD_SIZE)]
    key_gradient = key_gradient.at[:rows_per_step].add(
        jnp.einsum(
            "ngqk,qngd->knd", grad_scores, heads_of_query, preferred_element_type=jnp.float32
        )
    )
    value_gradient = value_gradient.at[:rows_per_step].add(
        jnp.einsum(
            "ngqk,qngd->knd",
            chances.astype(jnp.bfloat16),
            head_gradient,
            preferred_element_type=jnp.float32,
        )
    )
    return (
        jnp.concatenate(query_parts, axis=0),
        key_gradient.reshape(SLOT_PLACES, KEY_VALUE_HEADS * HEAD_SIZE),
        value_gradient.reshape(SLOT_PLACES, KEY_VALUE_HEADS * HEAD_SIZE),
    )


def apply_projection(value_rows, weight_matrix):
    return jnp.einsum("avi,iq->avq", value_rows, weight_matrix, preferred_element_type=jnp.float32)


def back_project(gradient_rows, weight_matrix):
    return jnp.einsum(
        "zxt,wt->zxw", gradient_rows, weight_matrix, preferred_element_type=jnp.float32
    )


def weight_term(left_operand, right_operand):
    return jnp.einsum(
        "cmx,cmw->xw", left_operand, right_operand, preferred_element_type=jnp.float32
    )


def gating(gate_in, up_in):
    return jax.nn.silu(gate_in) * up_in


def on_device(
    block_input,
    lengths,
    attention_gain,
    query_weight,
    key_matrix,
    value_matrix,
    output_weight,
    mlp_gain,
    gate_weight,
    up_weight,
    down_weight,
    cotangent,
):
    part_query, part_key, part_value, part_output, part_gate, part_up, part_down = (
        lax.all_gather(query_weight, "fsdp", axis=1, tiled=True),
        lax.all_gather(key_matrix, "fsdp", axis=1, tiled=True),
        lax.all_gather(value_matrix, "fsdp", axis=1, tiled=True),
        lax.all_gather(output_weight, "fsdp", axis=1, tiled=True),
        lax.all_gather(gate_weight, "fsdp", axis=1, tiled=True),
        lax.all_gather(up_weight, "fsdp", axis=1, tiled=True),
        lax.all_gather(down_weight, "fsdp", axis=1, tiled=True),
    )
    full_weights = (
        lax.all_gather(part_query, "dp", axis=0, tiled=True),
        lax.all_gather(part_key, "dp", axis=0, tiled=True),
        lax.all_gather(part_value, "dp", axis=0, tiled=True),
        lax.all_gather(part_output, "dp", axis=0, tiled=True),
        lax.all_gather(part_gate, "dp", axis=0, tiled=True),
        lax.all_gather(part_up, "dp", axis=0, tiled=True),
        lax.all_gather(part_down, "dp", axis=0, tiled=True),
    )
    full_query, complete_key, full_value, full_output, full_gate, full_up, full_down = full_weights
    places = jnp.arange(SLOT_PLACES, dtype=jnp.int32)
    is_valid = (places[None, :] < lengths[:, None])[..., None]
    stream = block_input.astype(jnp.float32)
    kept = []
    totals = []
    for repeat in range(2):
        normalized = rms_scale(stream, attention_gain).astype(jnp.bfloat16)
        query_rows = apply_rotation(
            apply_projection(normalized, full_query), QUERY_HEADS, 1.0
        ).astype(jnp.bfloat16)
        rotated_keys = apply_rotation(
            apply_projection(normalized, complete_key), KEY_VALUE_HEADS, 1.0
        ).astype(jnp.bfloat16)
        value_rows = apply_projection(normalized, full_value).astype(jnp.bfloat16)
        attended, log_sums = lax.map(
            attend_forward, (query_rows, rotated_keys, value_rows, lengths)
        )
        attended = attended.astype(jnp.bfloat16)
        attn_branch = apply_projection(attended, full_output)
        middle = stream + attn_branch
        normed_mlp = rms_scale(middle, mlp_gain).astype(jnp.bfloat16)
        gate_value = apply_projection(normed_mlp, full_gate)
        upward = apply_projection(normed_mlp, full_up)
        hidden = gating(gate_value, upward).astype(jnp.bfloat16)
        mlp_branch = apply_projection(hidden, full_down)
        for branch in (stream, attn_branch, mlp_branch):
            totals.append(jnp.sum(jnp.where(is_valid, branch * branch, 0.0)))
        kept.append(
            (
                stream,
                normalized,
                query_rows,
                rotated_keys,
                value_rows,
                log_sums,
                attended,
                middle,
                normed_mlp,
                gate_value,
                upward,
                hidden,
            )
        )
        stream = middle + mlp_branch
    block_output = jnp.where(is_valid, stream, 0.0).astype(jnp.bfloat16)
    local_totals = jnp.stack(totals)
    local_count = jnp.sum(lengths).astype(jnp.float32)
    global_totals, global_count = lax.psum((local_totals, local_count), ("dp", "fsdp"))
    grad_stream = jnp.where(is_valid, cotangent.astype(jnp.float32), 0.0)
    total_query = 0.0
    total_key = 0.0
    total_value = 0.0
    total_output = 0.0
    total_gate = 0.0
    total_up = 0.0
    total_down = 0.0
    total_attn_gain = 0.0
    total_mlp_gain = 0.0
    for repeat in (1, 0):
        (
            stream,
            normalized,
            query_rows,
            rotated_keys,
            value_rows,
            log_sums,
            attended,
            middle,
            normed_mlp,
            gate_value,
            upward,
            hidden,
        ) = kept[repeat]
        grad_low = grad_stream.astype(jnp.bfloat16)
        total_down = total_down + weight_term(hidden, grad_low)
        grad_hidden = back_project(grad_low, full_down)
        unused_value, gating_back = jax.vjp(gating, gate_value, upward)
        grad_gate_value, grad_upward = gating_back(grad_hidden)
        grad_gate_value = grad_gate_value.astype(jnp.bfloat16)
        grad_upward = grad_upward.astype(jnp.bfloat16)
        total_gate = total_gate + weight_term(normed_mlp, grad_gate_value)
        total_up = total_up + weight_term(normed_mlp, grad_upward)
        grad_normed_mlp = back_project(grad_gate_value, full_gate) + back_project(
            grad_upward, full_up
        )
        unused_value, norm_back = jax.vjp(rms_scale, middle, mlp_gain)
        grad_middle, grad_gain = norm_back(grad_normed_mlp)
        total_mlp_gain = total_mlp_gain + grad_gain
        grad_stream = grad_stream + grad_middle
        grad_low = grad_stream.astype(jnp.bfloat16)
        total_output = total_output + weight_term(attended, grad_low)
        grad_attended = back_project(grad_low, full_output).astype(jnp.bfloat16)
        grad_queries, keys_gradient, grad_values = lax.map(
            attend_backward,
            (query_rows, rotated_keys, value_rows, grad_attended, log_sums, lengths),
        )
        grad_query_proj = apply_rotation(grad_queries, QUERY_HEADS, -1.0).astype(jnp.bfloat16)
        key_projection_gradient = apply_rotation(keys_gradient, KEY_VALUE_HEADS, -1.0).astype(
            jnp.bfloat16
        )
        grad_value_proj = grad_values.astype(jnp.bfloat16)
        total_query = total_query + weight_term(normalized, grad_query_proj)
        total_key = total_key + weight_term(normalized, key_projection_gradient)
        total_value = total_value + weight_term(normalized, grad_value_proj)
        grad_normed = (
            back_project(grad_query_proj, full_query)
            + back_project(key_projection_gradient, complete_key)
            + back_project(grad_value_proj, full_value)
        )
        unused_value, norm_back = jax.vjp(rms_scale, stream, attention_gain)
        grad_before, grad_gain = norm_back(grad_normed)
        total_attn_gain = total_attn_gain + grad_gain
        grad_stream = grad_stream + grad_before
    part_query, part_key, part_value, part_output, part_gate, part_up, part_down = (
        lax.psum_scatter(total_query, "dp", scatter_dimension=0, tiled=True),
        lax.psum_scatter(total_key, "dp", scatter_dimension=0, tiled=True),
        lax.psum_scatter(total_value, "dp", scatter_dimension=0, tiled=True),
        lax.psum_scatter(total_output, "dp", scatter_dimension=0, tiled=True),
        lax.psum_scatter(total_gate, "dp", scatter_dimension=0, tiled=True),
        lax.psum_scatter(total_up, "dp", scatter_dimension=0, tiled=True),
        lax.psum_scatter(total_down, "dp", scatter_dimension=0, tiled=True),
    )
    sharded_grads = (
        lax.psum_scatter(part_query, "fsdp", scatter_dimension=1, tiled=True),
        lax.psum_scatter(part_key, "fsdp", scatter_dimension=1, tiled=True),
        lax.psum_scatter(part_value, "fsdp", scatter_dimension=1, tiled=True),
        lax.psum_scatter(part_output, "fsdp", scatter_dimension=1, tiled=True),
        lax.psum_scatter(part_gate, "fsdp", scatter_dimension=1, tiled=True),
        lax.psum_scatter(part_up, "fsdp", scatter_dimension=1, tiled=True),
        lax.psum_scatter(part_down, "fsdp", scatter_dimension=1, tiled=True),
    )
    grad_query, grad_key, grad_value, grad_output, grad_gate, grad_up, grad_down = sharded_grads
    grad_attention_gain, grad_mlp_gain = lax.psum((total_attn_gain, total_mlp_gain), ("dp", "fsdp"))
    stream_rms = jnp.sqrt(global_totals.reshape(2, 3) / (global_count * MODEL_WIDTH))
    return (
        block_output,
        grad_stream,
        grad_attention_gain,
        grad_query,
        grad_key,
        grad_value,
        grad_output,
        grad_mlp_gain,
        grad_gate,
        grad_up,
        grad_down,
        stream_rms,
    )


def solution(mesh):
    in_specs = (
        P(("dp", "fsdp"), None, None),
        P(("dp", "fsdp")),
        P(),
        P("dp", "fsdp"),
        P("dp", "fsdp"),
        P("dp", "fsdp"),
        P("dp", "fsdp"),
        P(),
        P("dp", "fsdp"),
        P("dp", "fsdp"),
        P("dp", "fsdp"),
        P(("dp", "fsdp"), None, None),
    )
    out_specs = (
        P(("dp", "fsdp"), None, None),
        P(("dp", "fsdp"), None, None),
        P(),
        P("dp", "fsdp"),
        P("dp", "fsdp"),
        P("dp", "fsdp"),
        P("dp", "fsdp"),
        P(),
        P("dp", "fsdp"),
        P("dp", "fsdp"),
        P("dp", "fsdp"),
        P(),
    )
    return jax.shard_map(
        on_device, mesh=mesh, in_specs=in_specs, out_specs=out_specs, check_vma=False
    )
```

profile of v0, /device:TPU:0, one launch (start us, length us, event | category | flops | bytes accessed | tf_op | source)
XLA Modules:
  0.0 1073.0 jit_solution(6529634537725805090)
XLA Ops:
  7.2 33.6 %all-gather = bf16[8,192,144]{1,2,0:T(8,128)(2,1)S(1)} all-gather(bf16[1,192,144]{1,2,0:T(8,128)(2,1)} %bitcast.410), channel_id=1, replica_groups=mesh['dp'=4,'fsdp'=8] {'fsdp'}, dimensions={0}, use_global_device_ids=true | all-gather | bytes 497664 | tf_op jit(solution)/shard_map/all_gather | solution.py:169
  42.3 31.5 %all-gather.1 = bf16[8,192,144]{1,2,0:T(8,128)(2,1)S(1)} all-gather(bf16[1,192,144]{1,2,0:T(8,128)(2,1)S(1)} %bitcast.411), channel_id=1, replica_groups=mesh['dp'=4,'fsdp'=8] {'fsdp'}, dimensions={0}, use_global_device_ids=true | all-gather | bytes 497664 | tf_op jit(solution)/shard_map/all_gather | solution.py:170
  75.3 33.1 %all_gather.54 = bf16[384,576]{0,1:T(8,128)(2,1)} all-gather(bf16[384,72]{0,1:T(8,128)(2,1)S(1)} %copy-done.89), channel_id=1, replica_groups=mesh['dp'=4,'fsdp'=8] {'fsdp'}, dimensions={1}, use_global_device_ids=true | all-gather | bytes 497664 | tf_op jit(solution)/shard_map/all_gather | solution.py:171
  109.3 31.0 %all_gather.46 = bf16[144,576]{0,1:T(8,128)(2,1)S(1)} all-gather(bf16[144,72]{0,1:T(8,128)(2,1)S(1)} %copy.68), channel_id=1, replica_groups=mesh['dp'=4,'fsdp'=8] {'fsdp'}, dimensions={1}, use_global_device_ids=true | all-gather | bytes 186624 | tf_op jit(solution)/shard_map/all_gather | solution.py:165
  140.5 8.3 all_gather.47
  150.1 30.5 %all_gather.44 = bf16[144,192]{0,1:T(8,128)(2,1)S(1)} all-gather(bf16[144,24]{0,1:T(8,128)(2,1)S(1)} %copy-done.101), channel_id=1, replica_groups=mesh['dp'=4,'fsdp'=8] {'fsdp'}, dimensions={1}, use_global_device_ids=true | all-gather | bytes 62208 | tf_op jit(solution)/shard_map/all_gather | solution.py:166
  180.7 5.9 all_gather.45
  189.1 30.5 %all_gather.42 = bf16[144,192]{0,1:T(8,128)(2,1)S(1)} all-gather(bf16[144,24]{0,1:T(8,128)(2,1)S(1)} %copy-done.102), channel_id=1, replica_groups=mesh['dp'=4,'fsdp'=8] {'fsdp'}, dimensions={1}, use_global_device_ids=true | all-gather | bytes 62208 | tf_op jit(solution)/shard_map/all_gather | solution.py:167
  219.8 5.9 all_gather.43
  229.3 2.3 copy-done
  231.6 1.7 fusion.41
  233.4 30.8 %all_gather.48 = bf16[144,576]{0,1:T(8,128)(2,1)S(1)} all-gather(bf16[144,72]{0,1:T(8,128)(2,1)S(1)} %copy.72), channel_id=1, replica_groups=mesh['dp'=4,'fsdp'=8] {'fsdp'}, dimensions={1}, use_global_device_ids=true | all-gather | bytes 186624 | tf_op jit(solution)/shard_map/all_gather | solution.py:168
  264.4 7.6 all_gather.49
  272.1 1.7 multiply_reduce_fusion.1
  274.0 5.0 fusion.138
  279.0 6.3 multiply_convert_fusion.3
  285.3 4.5 multiply_reduce_fusion.2
  296.0 1.7 fusion.40
  297.7 1.7 multiply_reduce_fusion
  302.6 1.8 fusion.139
  304.4 2.8 multiply_convert_fusion.1
  309.0 1.9 fusion.59
  310.9 2.5 fusion.53
  314.1 5.0 fusion.142
  319.1 2.3 fusion.70
  321.4 14.9 %fusion.43 = f32[1,512,3,64]{1,3,2,0:T(8,128)} fusion(bf16[512,3,3,64]{0,3,2,1:T(8,128)(2,1)} %bitcast.379, f32[3,512,512,3]{2,1,3,0:T(8,128)} %fusion.142, f32[3,3,512,512]{2,3,1,0:T(8,128)} %copy-done.1, f32[3,3,512]{2,1,0:T(4,128)} %copy-done.87, pred[512,512]{0,1:T(8,128)(4,1)} %copy-done.8), kind=kOutput, calls=%fused_computation.87 | convolution fusion | flops 320869376 | bytes 20137984 | tf_op jit(solution)/shard_map/while/body/eval_jaxpr/ngqk,qngd->knd/dot_general | solution.py:111
  336.3 15.3 %fusion.32 = f32[3,64,3,512]{3,1,2,0:T(8,128)} fusion(f32[3,512,512,3]{2,1,3,0:T(8,128)} %fusion.142, f32[3,3,512,512]{2,3,1,0:T(8,128)} %copy-done.1, f32[3,3,512]{2,1,0:T(4,128)} %copy-done.87, pred[512,512]{0,1:T(8,128)(4,1)} %copy-done.8, bf16[1,512,3,32]{1,3,2,0:T(8,128)(2,1)} %copy-done.76, bf16[1,512,3,32]{1,3,2,0:T(8,128)(2,1)} %copy-done.75), kind=kOutput, calls=%fused_computation.53 | convolution fusion | flops 321262592 | bytes 20531200 | tf_op jit(solution)/shard_map/while/body/eval_jaxpr/ngqk,knd->qngd/dot_general | solution.py:106
  351.7 1.8 fusion.82
  360.4 2.5 multiply_convert_fusion
  366.0 2.0 fusion.58
  369.0 1.8 convolution_add_fusion.3
  373.4 5.0 fusion.144
  378.4 15.8 %fusion.35 = f32[3,64,3,512]{3,1,2,0:T(8,128)} fusion(f32[3,512,512,3]{2,1,3,0:T(8,128)} %fusion.144, f32[3,3,512,512]{2,3,1,0:T(8,128)} %copy-done, f32[3,3,512]{2,1,0:T(4,128)S(1)} %log_add_fusion, pred[512,512]{0,1:T(8,128)(4,1)S(1)} %copy-done.9, bf16[1,512,3,32]{1,3,2,0:T(8,128)(2,1)S(1)} %copy-done.74, bf16[1,512,3,32]{1,3,2,0:T(8,128)(2,1)S(1)} %copy-done.72), kind=kOutput, calls=%fused_computation.56 | convolution fusion | flops 321262592 | bytes 20531200 | tf_op jit(solution)/shard_map/while/body/eval_jaxpr/ngqk,knd->qngd/dot_general | solution.py:106
  396.6 1.9 convolution_add_fusion.4
  398.8 2.8 fusion.146
  401.6 2.9 convolution_add_fusion.1
  404.6 2.8 fusion.145
  407.4 2.9 convolution_add_fusion.2
  411.4 15.0 %fusion.42 = f32[1,512,3,64]{1,3,2,0:T(8,128)} fusion(bf16[512,3,3,64]{0,3,2,1:T(8,128)(2,1)S(1)} %bitcast.377, f32[3,512,512,3]{2,1,3,0:T(8,128)} %fusion.144, f32[3,3,512,512]{2,3,1,0:T(8,128)} %copy-done, f32[3,3,512]{2,1,0:T(4,128)} %copy-done.86, pred[512,512]{0,1:T(8,128)(4,1)S(1)} %copy-done.9), kind=kOutput, calls=%fused_computation.86 | convolution fusion | flops 320869376 | bytes 20137984 | tf_op jit(solution)/shard_map/while/body/eval_jaxpr/ngqk,qngd->knd/dot_general | solution.py:111
  427.5 5.3 fusion.67
  437.3 2.8 fusion.100
  440.1 2.9 convolution_add_fusion
  443.1 2.0 copy.107
  445.2 2.0 copy.101
  447.3 25.6 %reduce-scatter.39.cloned.1.call-done = f32[144,1536]{1,0:T(8,128)} async-done(((f32[576,1536]{1,0:T(8,128)}), f32[144,1536]{1,0:T(8,128)}) %reduce-scatter.39.cloned.1.call-update) | async-done | bytes 884752 | tf_op jit(solution)/shard_map/reduce_scatter | solution.py:302
  472.9 2.8 copy.111
  475.8 40.3 %reduce-scatter.37.cloned.1.call-done = f32[144,1536]{1,0:T(8,128)} async-done(((f32[576,1536]{1,0:T(8,128)}), f32[144,1536]{1,0:T(8,128)}) %reduce-scatter.37.cloned.1.call-update) | async-done | bytes 884752 | tf_op jit(solution)/shard_map/reduce_scatter | solution.py:301
  516.1 2.8 copy.109
  519.0 21.7 %reduce-scatter.33.cloned.1.call-done = f32[144,192]{1,0:T(8,128)} async-done(((f32[576,192]{1,0:T(8,128)}), f32[144,192]{1,0:T(8,128)}) %reduce-scatter.33.cloned.1.call-update) | async-done | bytes 110608 | tf_op jit(solution)/shard_map/reduce_scatter | solution.py:299
  540.7 1.7 copy.105
  542.5 22.8 %reduce-scatter.31.cloned.1.call-done = f32[144,192]{1,0:T(8,128)} async-done(((f32[576,192]{1,0:T(8,128)}), f32[144,192]{1,0:T(8,128)}) %reduce-scatter.31.cloned.1.call-update) | async-done | bytes 110608 | tf_op jit(solution)/shard_map/reduce_scatter | solution.py:298
  565.3 1.7 copy.103
  567.3 40.9 %reduce-scatter.41.cloned.1.call-done = f32[384,576]{0,1:T(8,128)} async-done(((f32[1536,576]{0,1:T(8,128)}), f32[384,576]{0,1:T(8,128)}) %reduce-scatter.41.cloned.1.call-update) | async-done | bytes 884752 | tf_op jit(solution)/shard_map/reduce_scatter | solution.py:303
  613.2 3.9 stack.27
  617.1 39.7 %all-reduce.1 = (f32[576]{0:T(1024)}, f32[576]{0:T(1024)}, f32[6]{0:T(128)S(1)}, f32[]{:T(128)}) all-reduce(f32[576]{0:T(1024)S(1)} %add.289, f32[576]{0:T(1024)S(1)} %add.296, f32[6]{0:T(128)S(1)} %stack.27, f32[]{:T(128)S(6)} %convert_element_type.331), channel_id=1, replica_groups=mesh['dp'=4,'fsdp'=8] {'dp','fsdp'}, use_global_device_ids=true, to_apply=%region_16.17 | all-reduce | flops 1159 | bytes 9272 | tf_op jit(solution)/shard_map/psum | solution.py:315
  659.5 14.6 %reduce-scatter.49.cloned.1.call-done = f32[72,144]{1,0:T(8,128)} async-done(((f32[576,144]{1,0:T(8,128)}), f32[72,144]{1,0:T(8,128)}) %reduce-scatter.49.cloned.1.call-update) | async-done | bytes 41488
  675.8 62.6 %reduce-scatter.43.cloned.1.call-done = f32[72,144]{1,0:T(8,128)} async-done(((f32[576,144]{1,0:T(8,128)}), f32[72,144]{1,0:T(8,128)}) %reduce-scatter.43.cloned.1.call-update) | async-done | bytes 41488
  740.0 66.2 %reduce-scatter.53.cloned.1.call-done = f32[192,144]{1,0:T(8,128)} async-done(((f32[1536,144]{1,0:T(8,128)}), f32[192,144]{1,0:T(8,128)}) %reduce-scatter.53.cloned.1.call-update) | async-done | bytes 110608
  806.2 1.7 copy.112
  807.9 65.5 %reduce-scatter.51.cloned.1.call-done = f32[192,144]{1,0:T(8,128)} async-done(((f32[1536,144]{1,0:T(8,128)}), f32[192,144]{1,0:T(8,128)}) %reduce-scatter.51.cloned.1.call-update) | async-done | bytes 110608
  873.4 1.7 copy.110
  875.1 62.3 %reduce-scatter.47.cloned.1.call-done = f32[24,144]{1,0:T(8,128)} async-done(((f32[192,144]{1,0:T(8,128)}), f32[24,144]{1,0:T(8,128)}) %reduce-scatter.47.cloned.1.call-update) | async-done | bytes 13840
  937.4 64.1 %reduce-scatter.45.cloned.1.call-done = f32[24,144]{1,0:T(8,128)} async-done(((f32[192,144]{1,0:T(8,128)}), f32[24,144]{1,0:T(8,128)}) %reduce-scatter.45.cloned.1.call-update) | async-done | bytes 13840
  1001.5 64.5 %reduce-scatter.55.cloned.1.call-done = f32[384,72]{0,1:T(8,128)} async-done(((f32[384,576]{0,1:T(8,128)}), f32[384,72]{0,1:T(8,128)}) %reduce-scatter.55.cloned.1.call-update) | async-done | bytes 110608
  (344 shorter events, 56.2 us)
Async XLA Ops:
  7.2 266.8 %all-gather.6.cloned.1.call-start = ((), (), s32[]{:S(2)}) async-start(), calls=%async_computation.14 | async-start | bytes 2211840 | tf_op jit(solution)/shard_map/all_gather | solution.py:178
  7.2 35.1 %copy-start.88 = (bf16[144,192]{1,0:T(8,128)(2,1)S(1)}, bf16[144,192]{1,0:T(8,128)(2,1)}, u32[]{:S(2)}) copy-start(bf16[144,192]{1,0:T(8,128)(2,1)} %param.37) | copy-start | bytes 165892
  42.2 236.7 %all-gather.8.cloned.1.call-start = ((), (), s32[]{:S(2)}) async-start(), calls=%async_computation.15 | async-start | bytes 2211840 | tf_op jit(solution)/shard_map/all_gather | solution.py:179
  42.3 33.0 %copy-start.89 = (bf16[384,72]{0,1:T(8,128)(2,1)S(1)}, bf16[384,72]{0,1:T(8,128)(2,1)}, u32[]{:S(2)}) copy-start(bf16[384,72]{0,1:T(8,128)(2,1)} %param.38) | copy-start | bytes 165892
  73.8 34.7 %copy-start.2 = (bf16[1,512,576]{1,2,0:T(8,128)(2,1)S(1)}, bf16[1,512,576]{1,2,0:T(8,128)(2,1)}, u32[]{:S(2)}) copy-start(bf16[1,512,576]{1,2,0:T(8,128)(2,1)} %param.28) | copy-start | bytes 1769476
  74.0 35.3 %copy-start.90 = (bf16[144,72]{1,0:T(8,128)(2,1)S(1)}, bf16[144,72]{1,0:T(8,128)(2,1)}, u32[]{:S(2)}) copy-start(bf16[144,72]{1,0:T(8,128)(2,1)} %param.31) | copy-start | bytes 62212
  75.2 210.1 %all-gather.10.cloned.1.call-start = ((), (), s32[]{:S(2)}) async-start(), calls=%async_computation.16 | async-start | bytes 2211840 | tf_op jit(solution)/shard_map/all_gather | solution.py:180
  108.4 334.7 %reduce-scatter.35.cloned.1.call-start = ((), (), s32[]{:S(2)}) async-start(), calls=%async_computation.20 | async-start | bytes 1843200 | tf_op jit(solution)/shard_map/reduce_scatter | solution.py:300
  140.3 9.7 copy-start.101
  148.8 38.8 %copy-start.12 = (bf16[576,576]{1,0:T(8,128)(2,1)}, bf16[576,576]{1,0:T(8,128)(2,1)S(1)}, u32[]{:S(2)}) copy-start(bf16[576,576]{1,0:T(8,128)(2,1)S(1)} %all_gather.47) | copy-start | bytes 1990660
  148.8 38.0 %copy-start.80 = (f32[576]{0:T(1024)S(1)}, f32[576]{0:T(1024)}, u32[]{:S(2)}) copy-start(f32[576]{0:T(1024)} %param.30) | copy-start | bytes 6916
  149.1 38.4 %copy-start.69 = (bf16[576,576]{1,0:T(8,128)(2,1)}, bf16[576,576]{1,0:T(8,128)(2,1)S(1)}, u32[]{:S(2)}) copy-start(bf16[576,576]{1,0:T(8,128)(2,1)S(1)} %copy.70) | copy-start | bytes 1990660
  150.1 142.7 %copy-start.25 = (f32[512,32]{0,1:T(8,128)}, f32[512,32]{0,1:T(8,128)S(1)}, u32[]{:S(2)}) copy-start(f32[512,32]{0,1:T(8,128)S(1)} %get-tuple-element.311) | copy-start | bytes 196612
  188.2 38.0 %copy-start.71 = (bf16[1,512,3,32]{1,3,2,0:T(8,128)(2,1)}, bf16[1,512,3,32]{1,3,2,0:T(8,128)(2,1)S(1)}, u32[]{:S(2)}) copy-start(bf16[1,512,3,32]{1,3,2,0:T(8,128)(2,1)S(1)} %get-tuple-element.307) | copy-start | bytes 294916
  188.2 38.0 %copy-start.73 = (bf16[1,512,3,32]{1,3,2,0:T(8,128)(2,1)}, bf16[1,512,3,32]{1,3,2,0:T(8,128)(2,1)S(1)}, u32[]{:S(2)}) copy-start(bf16[1,512,3,32]{1,3,2,0:T(8,128)(2,1)S(1)} %get-tuple-element.308) | copy-start | bytes 294916
  189.1 103.8 %copy-start.8 = (pred[512,512]{0,1:T(8,128)(4,1)}, pred[512,512]{0,1:T(8,128)(4,1)S(1)}, u32[]{:S(2)}) copy-start(pred[512,512]{0,1:T(8,128)(4,1)S(1)} %fusion.73) | copy-start | bytes 786436
  226.1 3.1 copy-start.81
  227.9 3.7 copy-start
  227.9 3.7 copy-start.78
  229.2 4.1 copy-start.84
  233.3 40.4 %copy-start.44 = (bf16[3,64,3,512]{3,1,2,0:T(8,128)(2,1)}, bf16[3,64,3,512]{3,1,2,0:T(8,128)(2,1)S(1)}, u32[]{:S(2)}) copy-start(bf16[3,64,3,512]{3,1,2,0:T(8,128)(2,1)S(1)} %fusion.41) | copy-start | bytes 1769476
  272.0 25.7 %copy-start.3 = (bf16[576,576]{1,0:T(8,128)(2,1)}, bf16[576,576]{1,0:T(8,128)(2,1)S(1)}, u32[]{:S(2)}) copy-start(bf16[576,576]{1,0:T(8,128)(2,1)S(1)} %all_gather.49) | copy-start | bytes 1990660
  273.8 5.2 copy-start.15
  273.8 5.2 copy-start.96
  273.8 5.2 copy-start.98
  273.9 5.0 copy-start.10
  294.6 24.5 %copy-start.1 = (f32[3,3,512,512]{2,3,1,0:T(8,128)}, f32[3,3,512,512]{2,3,1,0:T(8,128)S(1)}, u32[]{:S(2)}) copy-start(f32[3,3,512,512]{2,3,1,0:T(8,128)S(1)} %get-tuple-element.319) | copy-start | bytes 28311556
  296.0 23.1 %copy-start.87 = (f32[3,3,512]{2,1,0:T(4,128)}, f32[3,3,512]{2,1,0:T(4,128)S(1)}, u32[]{:S(2)}) copy-start(f32[3,3,512]{2,1,0:T(4,128)S(1)} %log_add_fusion.1) | copy-start | bytes 55300
  307.3 3.7 copy-start.18
  310.9 2.5 copy-start.4
  356.4 3.3 copy-start.112
  357.7 2.7 copy-start.51
  358.1 9.9 copy-start.6
  360.4 2.6 copy-start.108
  363.0 2.9 copy-start.110
  370.8 74.4 %reduce-scatter.29.cloned.1.call-start = ((), (), s32[]{:S(2)}) async-start(), calls=%async_computation.17 | async-start | bytes 1843200 | tf_op jit(solution)/shard_map/reduce_scatter | solution.py:297
  370.9 2.5 copy-start.82
  371.9 6.5 copy-start.86
  373.4 5.1 copy-start.9
  373.4 5.1 copy-start.72
  373.4 5.1 copy-start.74
  378.4 15.8 %copy-start.27 = (f32[512,32]{0,1:T(8,128)S(1)}, f32[512,32]{0,1:T(8,128)}, u32[]{:S(2)}) copy-start(f32[512,32]{0,1:T(8,128)} %copy-done.25) | copy-start | bytes 196612
  378.4 15.8 %copy-start.55 = (f32[512,32]{0,1:T(8,128)S(1)}, f32[512,32]{0,1:T(8,128)}, u32[]{:S(2)}) copy-start(f32[512,32]{0,1:T(8,128)} %get-tuple-element.309) | copy-start | bytes 196612
  398.5 3.1 copy-start.11
  398.5 74.4 %reduce-scatter.39.cloned.1.call-start = ((), (), s32[]{:S(2)}) async-start(), calls=%async_computation.22 | async-start | bytes 4423680 | tf_op jit(solution)/shard_map/reduce_scatter | solution.py:302
  398.8 2.8 copy-start.61
  404.5 111.5 %reduce-scatter.37.cloned.1.call-start = ((), (), s32[]{:S(2)}) async-start(), calls=%async_computation.21 | async-start | bytes 4423680 | tf_op jit(solution)/shard_map/reduce_scatter | solution.py:301
  404.6 2.8 copy-start.59
  410.3 16.1 %copy-start.53 = (bf16[3,64,512]{2,1,0:T(8,128)(2,1)S(1)}, bf16[3,64,512]{2,1,0:T(8,128)(2,1)}, u32[]{:S(2)}) copy-start(bf16[3,64,512]{2,1,0:T(8,128)(2,1)} %fusion.70) | copy-start | bytes 589828
  410.4 130.3 %reduce-scatter.33.cloned.1.call-start = ((), (), s32[]{:S(2)}) async-start(), calls=%async_computation.19 | async-start | bytes 737280 | tf_op jit(solution)/shard_map/reduce_scatter | solution.py:299
  434.1 131.2 %reduce-scatter.31.cloned.1.call-start = ((), (), s32[]{:S(2)}) async-start(), calls=%async_computation.18 | async-start | bytes 737280 | tf_op jit(solution)/shard_map/reduce_scatter | solution.py:298
  437.2 2.9 copy-start.7
  437.2 171.0 %reduce-scatter.41.cloned.1.call-start = ((), (), s32[]{:S(2)}) async-start(), calls=%async_computation.23 | async-start | bytes 4423680 | tf_op jit(solution)/shard_map/reduce_scatter | solution.py:303
  437.3 2.8 copy-start.62
  443.0 231.1 %reduce-scatter.49.cloned.1.call-start = ((), (), s32[]{:S(2)}) async-start(), calls=%async_computation.27 | async-start | bytes 663552
  445.1 293.2 %reduce-scatter.43.cloned.1.call-start = ((), (), s32[]{:S(2)}) async-start(), calls=%async_computation.24 | async-start | bytes 663552
  447.3 358.9 %reduce-scatter.53.cloned.1.call-start = ((), (), s32[]{:S(2)}) async-start(), calls=%async_computation.29 | async-start | bytes 1769472
  475.7 397.6 %reduce-scatter.51.cloned.1.call-start = ((), (), s32[]{:S(2)}) async-start(), calls=%async_computation.28 | async-start | bytes 1769472
  518.9 89.3 %copy-start.14 = (bf16[576,576]{1,0:T(8,128)(2,1)S(1)}, bf16[576,576]{1,0:T(8,128)(2,1)}, u32[]{:S(2)}) copy-start(bf16[576,576]{1,0:T(8,128)(2,1)} %copy-done.12) | copy-start | bytes 1990660
  518.9 89.3 %copy-start.22 = (bf16[1,512,9,64]{1,3,2,0:T(8,128)(2,1)S(1)}, bf16[1,512,9,64]{1,3,2,0:T(8,128)(2,1)}, u32[]{:S(2)}) copy-start(bf16[1,512,9,64]{1,3,2,0:T(8,128)(2,1)} %copy-done.21) | copy-start | bytes 1769476
  518.9 418.5 %reduce-scatter.47.cloned.1.call-start = ((), (), s32[]{:S(2)}) async-start(), calls=%async_computation.26 | async-start | bytes 221184
  542.4 459.1 %reduce-scatter.45.cloned.1.call-start = ((), (), s32[]{:S(2)}) async-start(), calls=%async_computation.25 | async-start | bytes 221184
  567.0 499.0 %reduce-scatter.55.cloned.1.call-start = ((), (), s32[]{:S(2)}) async-start(), calls=%async_computation.30 | async-start | bytes 995328
  612.0 46.2 %copy-start.95 = (f32[512]{0:T(512)S(1)}, f32[512]{0:T(512)}, u32[]{:S(2)}) copy-start(f32[512]{0:T(512)} %copy-done.94) | copy-start | bytes 6148
  (66 other events, 96.2 us)
Sparse Core Ops, SparseCore 0:
  42.4 21.7 all-gather.5
  75.4 22.0 all-gather.7
  108.5 22.2 all-gather.9
  370.9 28.8 reduce-scatter.34
  402.5 27.5 reduce-scatter.28
  432.4 40.4 reduce-scatter.38
  475.6 40.4 reduce-scatter.36
  518.6 22.0 reduce-scatter.32
  543.2 22.0 reduce-scatter.30
  567.7 40.4 reduce-scatter.40
  611.8 62.2 reduce-scatter.48
  677.3 61.0 reduce-scatter.42
  742.2 63.9 reduce-scatter.52
  809.5 63.8 reduce-scatter.50
  877.4 59.9 reduce-scatter.46
  941.4 60.0 reduce-scatter.44
  1005.7 60.2 reduce-scatter.54
where the time goes:
time: 1080 us; the launch traced here: 1070 us
  waiting for transfers between devices  552 us (51%)
  blocking collectives  288 us (27%)
  matrix products  157 us (15%)
  local copies, waits for them, and re-layouts  46.9 us (4%)
  between operations  17.3 us (2%)
  other arithmetic  11.2 us (1%)
    unnamed x24, waiting for transfers between devices  400 us
    unnamed x240, local copies, waits for them, and re-layouts  41 us
    reduce_scatter x1, waiting for transfers between devices, on_device(): lax.psum_scatter(total_down, 'dp', scatter_dimension=0, tiled=True)  40.9 us
    reduce_scatter x1, waiting for transfers between devices, on_device(): lax.psum_scatter(total_gate, 'dp', scatter_dimension=0, tiled=True)  40.3 us
    psum x1, blocking collectives, on_device(): lax.psum((total_attn_gain, total_mlp_gain), ('dp', 'fsdp'))  39.7 us
    all_gather x1, blocking collectives, on_device(): lax.all_gather(gate_weight, 'fsdp', axis=1, tiled=True)  33.6 us
    all_gather x1, blocking collectives, on_device(): lax.all_gather(down_weight, 'fsdp', axis=1, tiled=True)  33.1 us
    all_gather x1, blocking collectives, on_device(): lax.all_gather(up_weight, 'fsdp', axis=1, tiled=True)  31.5 us
  transfers between devices with their start and end apart: 17, of which 12 were waited for; matrix products, arithmetic and copies ran while one was open for 11% of the time, Pallas kernels for 0%

commit v1 on v0

v1 whole, which is shorter than its diff:
```python
import functools
import jax
import jax.numpy as jnp
import numpy as np
from jax import lax
from jax.experimental import pallas as pl
from jax.experimental.pallas import tpu as pltpu
from jax.sharding import PartitionSpec as P

D = 576
NQ = 9
NK = 3
GROUP = NQ // NK
H = 64
HALF = H // 2
FF = 1536
T = 512
NF = 8
QB = D // NF
KB = NK * H // NF
FB = FF // NF
OB = 80
EPS = 1e-05
ROPE_BASE = 10000.0
SCALE = H ** (-0.5)
NEG = -1e30
BLK = 256
VMEM_LIMIT = 63 * 2**20
BF = jnp.bfloat16
F32 = jnp.float32


def dot(a, b, ca, cb):
    return lax.dot_general(a, b, (((ca,), (cb,)), ((), ())), preferred_element_type=F32)


def rope_tables():
    inverse = ROPE_BASE ** (-(2.0 * np.arange(HALF, dtype=np.float64)) / H)
    angles = inverse[:, None] * np.arange(T, dtype=np.float64)[None, :]
    return np.cos(angles).astype(np.float32), np.sin(angles).astype(np.float32)


def parts_of(row):
    hi = row.astype(BF).astype(F32)
    rest = row - hi
    mid = rest.astype(BF).astype(F32)
    return [hi, mid, rest - mid]


def lane_tiles():
    return [slice(128 * i, 128 * i + 128) for i in range(T // 128)]


class Work:
    def __init__(self, order, refs):
        self.order = order
        self.__dict__.update(refs)

    def start(self):
        count = self.length[0]
        place = lax.broadcasted_iota(jnp.int32, (8, T), 1)
        valid = (place < count).astype(F32)
        self.valid[...] = valid
        for ts in lane_tiles():
            self.S[0, :, ts] = self.x[ts, :].astype(F32).T
            self.G[:, ts] = self.ct[ts, :].astype(F32).T * valid[0:1, ts]
        self.gacc[...] = jnp.zeros_like(self.gacc)
        self.QA[:, :, H:, :] = jnp.zeros((2, NQ, H, T), BF)
        self.DOA[:, H:, :] = jnp.zeros((NQ, H, T), BF)

    def norm(self, src, r, gain, dst, rho_ref, row):
        for ts in lane_tiles():
            v = src[r, :, ts]
            total = jnp.sum(v * v, axis=0, keepdims=True)
            if row is not None:
                self.stat[row : row + 1, ts] = total
            rho = lax.rsqrt(total * (1.0 / D) + EPS)
            rho_ref[r, 0:1, ts] = rho
            dst[r, :, ts] = (v * rho * gain[...]).astype(BF)

    def natural_rows(self, ref, base, width, first, count):
        pieces = []
        row = first
        while row < first + count:
            f, i = row // width, row % width
            n = min(width - i, first + count - row)
            at = 128 * self.order.index(f) + base + i
            pieces.append(ref[at : at + n, :])
            row += n
        return pieces[0] if len(pieces) == 1 else jnp.concatenate(pieces, axis=0)

    def project(self, r):
        self.norm(self.S, r, self.ga, self.XA, self.rhoA, 3 * r)
        for c in range(2):
            cs = slice(512 * c, 512 * c + 512)
            self.Y[cs, :] = dot(self.WA[:, cs], self.XA[r], 0, 0)
        cos, sin = self.cos[...], self.sin[...]
        one = jnp.ones((1, T), F32)
        place = lax.broadcasted_iota(jnp.int32, (1, T), 1)
        bias = jnp.where(place < self.length[0], 0.0, NEG)
        for h in range(NQ + NK):
            base, width, at = (0, QB, h) if h < NQ else (QB, KB, h - NQ)
            a = self.natural_rows(self.Y, base, width, H * at, HALF)
            b = self.natural_rows(self.Y, base, width, H * at + HALF, HALF)
            first, second = a * cos - b * sin, b * cos + a * sin
            if h < NQ:
                self.QA[r, h, 0:HALF, :] = (first * SCALE).astype(BF)
                self.QA[r, h, HALF:H, :] = (second * SCALE).astype(BF)
                self.QA[r, h, H : H + 16, :] = jnp.concatenate([one, jnp.zeros((15, T), F32)], axis=0).astype(BF)
            else:
                g = h - NQ
                key = jnp.concatenate([first, second], axis=0)
                self.KT[r, g] = key.astype(BF)
                v = jnp.concatenate(
                    [
                        self.natural_rows(self.Y, QB + KB, KB, H * g, HALF),
                        self.natural_rows(self.Y, QB + KB, KB, H * g + HALF, HALF),
                    ],
                    axis=0,
                )
                self.VT[g] = v.astype(BF)
                ones3 = jnp.ones((3, T), F32)
                tail = jnp.zeros((H - 4, T), F32)
                ktall = jnp.concatenate([key, bias, ones3, tail], axis=0)
                vtall = jnp.concatenate([v, jnp.zeros((1, T), F32), ones3, tail], axis=0)
                for ts in lane_tiles():
                    self.KTOK[r, g, ts, :] = ktall[:, ts].T.astype(BF)
                    self.VTOK[r, g, ts, :] = vtall[:, ts].T.astype(BF)

    def diagonal(self):
        key = lax.broadcasted_iota(jnp.int32, (BLK, BLK), 0)
        query = lax.broadcasted_iota(jnp.int32, (BLK, BLK), 1)
        return key <= query

    def attend(self, r):
        low, high = slice(0, BLK), slice(BLK, T)

        def head(h, carry):
            g = h // GROUP
            allowed = self.diagonal()
            at = pl.ds(pl.multiple_of(h * H, H), H)
            s = dot(self.KTOK[r, g, low, :], self.QA[r, h, :, low], 1, 0)
            s = jnp.where(allowed, s, NEG)
            top = jnp.max(s, axis=0, keepdims=True)
            p = jnp.exp(s - top)
            total = jnp.sum(p, axis=0, keepdims=True)
            o = dot(self.VT[g, :, low], p.astype(BF), 1, 0)
            self.AT[r, at, low] = (o * (1.0 / total)).astype(BF)
            lse0 = top + jnp.log(total)
            s0 = dot(self.KTOK[r, g, low, :], self.QA[r, h, :, high], 1, 0)
            s1 = dot(self.KTOK[r, g, high, :], self.QA[r, h, :, high], 1, 0)
            s1 = jnp.where(allowed, s1, NEG)
            top = jnp.maximum(jnp.max(s0, axis=0, keepdims=True), jnp.max(s1, axis=0, keepdims=True))
            p0 = jnp.exp(s0 - top)
            p1 = jnp.exp(s1 - top)
            total = jnp.sum(p0, axis=0, keepdims=True) + jnp.sum(p1, axis=0, keepdims=True)
            o = dot(self.VT[g, :, low], p0.astype(BF), 1, 0) + dot(self.VT[g, :, high], p1.astype(BF), 1, 0)
            self.AT[r, at, high] = (o * (1.0 / total)).astype(BF)
            lse1 = top + jnp.log(total)
            lse = jnp.concatenate([lse0, lse1], axis=1)
            rows = [jnp.ones((1, T), F32)] + parts_of(-lse) + [jnp.zeros((12, T), F32)]
            self.QA[r, h, H : H + 16, :] = jnp.concatenate(rows, axis=0).astype(BF)
            return carry

        lax.fori_loop(0, NQ, head, 0)

    def out_project(self, r):
        for c in range(2):
            cs = slice(512 * c, 512 * c + 512)
            self.Y[cs, :] = dot(self.WO[:, cs], self.AT[r], 0, 0)
        squares = jnp.zeros((8, T), F32)
        for b in range(NF):
            f = self.order[b]
            y = self.Y[128 * b : 128 * b + QB, :]
            rows = slice(QB * f, QB * f + QB)
            self.M[r, rows, :] = self.S[r, rows, :] + y
            for i in range(QB // 8):
                squares = squares + y[8 * i : 8 * i + 8] * y[8 * i : 8 * i + 8]
        self.stat[3 * r + 1 : 3 * r + 2, :] = jnp.sum(squares, axis=0, keepdims=True)

    def mlp(self, r):
        self.norm(self.M, r, self.gm, self.XM, self.rhoM, None)

        def block(b, carry):
            f = 2 * lax.rem(b, 4) + b // 4 if self.order[1] == 2 else b
            cols = pl.ds(pl.multiple_of(2 * FB * b, 128), 2 * FB)
            gu = dot(self.WGU[:, cols], self.XM[r], 0, 0)
            gate, up = gu[:FB], gu[FB:]
            rows = pl.ds(pl.multiple_of(FB * f, 64), FB)
            self.GATE[r, rows, :] = gate.astype(BF)
            self.UP[r, rows, :] = up.astype(BF)
            self.HID[r, rows, :] = (gate * jax.nn.sigmoid(gate) * up).astype(BF)
            return carry

        lax.fori_loop(0, NF, block, 0)
        self.Y[0 : OB * NF, :] = dot(self.WDT[...], self.HID[r], 1, 0)
        squares = jnp.zeros((8, T), F32)
        for b in range(NF):
            f = self.order[b]
            y = self.Y[OB * b : OB * b + QB, :]
            rows = slice(QB * f, QB * f + QB)
            after = self.M[r, rows, :] + y
            if r == 0:
                self.S[1, rows, :] = after
            else:
                self.E[rows, :] = after
            for i in range(QB // 8):
                squares = squares + y[8 * i : 8 * i + 8] * y[8 * i : 8 * i + 8]
        self.stat[3 * r + 2 : 3 * r + 3, :] = jnp.sum(squares, axis=0, keepdims=True)

    def write_output(self):
        valid = self.valid[0:1, :]
        for ts in lane_tiles():
            v = jnp.where(valid[:, ts] > 0.0, self.E[:, ts], 0.0)
            self.out[ts, :] = v.T.astype(BF)

    def pack_grad(self, dst, width):
        for b in range(NF):
            f = self.order[b]
            v = self.G[QB * f : QB * f + QB, :]
            v = jnp.concatenate([v, jnp.zeros((width - QB, T), F32)], axis=0)
            dst[width * b : width * b + width, :] = v.astype(BF)

    def add_term(self, dst, index, value, r):
        if r == 0:
            value = value + dst[index].astype(F32)
        dst[index] = value.astype(dst.dtype)

    def norm_back(self, src, r, rho_ref, gain, slot):
        for ts in lane_tiles():
            e, v, rho = self.E[:, ts], src[r, :, ts], rho_ref[r, 0:1, ts]
            u = e * gain[...]
            mean = jnp.sum(u * v, axis=0, keepdims=True) * (1.0 / D)
            self.gacc[slot] += e * (v * rho)
            self.G[:, ts] = self.G[:, ts] + rho * (u - v * (rho * rho * mean))

    def mlp_back(self, r, links=None):
        self.pack_grad(self.GLD, OB)
        for c in range(2):
            cs = slice(768 * c, 768 * c + 768)
            self.add_term(self.DD, (slice(None), cs), dot(self.GLD[...], self.HID[r, cs, :], 1, 1), r)
        if links:
            links.sum_start("D")

        def block(z, carry):
            rows = pl.ds(pl.multiple_of(2 * FB * z, 128), 2 * FB)
            grad = dot(self.WDT[:, rows], self.GLD[...], 0, 0)
            gate = self.GATE[r, rows, :].astype(F32)
            up = self.UP[r, rows, :].astype(F32)
            sig = jax.nn.sigmoid(gate)
            dgate = grad * up * (sig * (1.0 + gate * (1.0 - sig)))
            dup = grad * (gate * sig)
            for k in range(2):
                b = z + 4 * k if self.order[1] == 2 else 2 * z + k
                self.DGU[pl.ds(pl.multiple_of(2 * FB * b, 128), FB), :] = dgate[FB * k : FB * k + FB].astype(BF)
                self.DGU[pl.ds(pl.multiple_of(2 * FB * b + FB, 64), FB), :] = dup[FB * k : FB * k + FB].astype(BF)
            return carry

        lax.fori_loop(0, 4, block, 0)
        for c in range(4):
            cs = slice(768 * c, 768 * c + 768)
            self.add_term(self.DG, (slice(None), cs), dot(self.XM[r], self.DGU[cs, :], 1, 1), r)
        if links:
            links.sum_start("G")
            links.sum_pair("D")
        self.E[...] = dot(self.WGU[...], self.DGU[...], 1, 0)
        self.norm_back(self.M, r, self.rhoM, self.gm, 1)

    def attend_back(self, r, links=None):
        self.pack_grad(self.GLO, 128)
        for c in range(2):
            cs = slice(512 * c, 512 * c + 512)
            self.add_term(self.DO, (slice(None), cs), dot(self.AT[r], self.GLO[cs, :], 1, 1), r)
        if links:
            links.sum_start("O")
            links.sum_pair("G")
            links.sum_cross("D")
        self.E[...] = dot(self.WO[...], self.GLO[...], 1, 0)
        for h in range(NQ):
            rows = slice(H * h, H * h + H)
            do = self.E[rows, :].astype(BF)
            self.DOA[h, 0:H, :] = do
            delta = jnp.sum(do.astype(F32) * self.AT[r, rows, :].astype(F32), axis=0, keepdims=True)
            rows = [jnp.zeros((1, T), F32)] + parts_of(-delta) + [jnp.zeros((12, T), F32)]
            self.DOA[h, H : H + 16, :] = jnp.concatenate(rows, axis=0).astype(BF)
        low, high = slice(0, BLK), slice(BLK, T)
        self.Y[D : D + 2 * NK * H, :] = jnp.zeros((2 * NK * H, T), F32)

        def head(h, carry):
            g = h // GROUP
            allowed = self.diagonal()
            at = pl.ds(pl.multiple_of(h * H, H), H)
            kat = pl.ds(pl.multiple_of(D + g * H, H), H)
            vat = pl.ds(pl.multiple_of(D + NK * H + g * H, H), H)
            q, do = self.QA[r, h], self.DOA[h]
            k0, k1 = self.KTOK[r, g, low, :], self.KTOK[r, g, high, :]
            v0, v1 = self.VTOK[r, g, low, :], self.VTOK[r, g, high, :]
            t0, t1 = self.KT[r, g, :, low], self.KT[r, g, :, high]

            p = jnp.where(allowed, jnp.exp(dot(k0, q[:, low], 1, 0)), 0.0)
            ds = (p * dot(v0, do[:, low], 1, 0)).astype(BF)
            p = p.astype(BF)
            self.Y[at, low] = dot(t0, ds, 1, 0) * SCALE
            dk0 = dot(q[0:H, low], ds, 1, 1)
            dv0 = dot(do[0:H, low], p, 1, 1)

            p = jnp.exp(dot(k0, q[:, high], 1, 0))
            ds = (p * dot(v0, do[:, high], 1, 0)).astype(BF)
            p = p.astype(BF)
            dq = dot(t0, ds, 1, 0)
            dk0 += dot(q[0:H, high], ds, 1, 1)
            dv0 += dot(do[0:H, high], p, 1, 1)

            p = jnp.where(allowed, jnp.exp(dot(k1, q[:, high], 1, 0)), 0.0)
            ds = (p * dot(v1, do[:, high], 1, 0)).astype(BF)
            p = p.astype(BF)
            self.Y[at, high] = (dq + dot(t1, ds, 1, 0)) * SCALE
            self.Y[kat, low] += dk0
            self.Y[vat, low] += dv0
            self.Y[kat, high] += dot(q[0:H, high], ds, 1, 1)
            self.Y[vat, high] += dot(do[0:H, high], p, 1, 1)
            return carry

        for g in range(NK):
            lax.fori_loop(GROUP * g, GROUP * g + GROUP, head, 0)
            if links and g == 0:
                links.sum_pair("O")
            if links and g == 1:
                links.sum_cross("G")
                links.sum_line("D")

    def project_back(self, r, links=None):
        cos, sin = self.cos[...], self.sin[...]
        for h in range(NQ + NK):
            first, second = slice(H * h, H * h + HALF), slice(H * h + HALF, H * h + H)
            a, b = self.Y[first, :], self.Y[second, :]
            self.Y[first, :] = a * cos + b * sin
            self.Y[second, :] = b * cos - a * sin
        for b in range(NF):
            f = self.order[b]
            rows = jnp.concatenate(
                [
                    self.Y[QB * f : QB * f + QB, :],
                    self.Y[D + KB * f : D + KB * f + KB, :],
                    self.Y[D + NK * H + KB * f : D + NK * H + KB * f + KB, :],
                    jnp.zeros((128 - QB - 2 * KB, T), F32),
                ],
                axis=0,
            )
            self.GLO[128 * b : 128 * b + 128, :] = rows.astype(BF)
        for c in range(2):
            cs = slice(512 * c, 512 * c + 512)
            self.add_term(self.DA, (slice(None), cs), dot(self.XA[r], self.GLO[cs, :], 1, 1), r)
        if links:
            links.sum_start("A")
            links.sum_cross("O")
            links.sum_line("G")
        self.E[...] = dot(self.WA[...], self.GLO[...], 1, 0)
        self.norm_back(self.S, r, self.rhoA, self.ga, 0)

    def write_grad(self):
        for ts in lane_tiles():
            self.gin[ts, :] = self.G[:, ts].T

    def small(self):
        valid = self.valid[0:1, :]
        rows = [jnp.sum(self.gacc[i].T, axis=0, keepdims=True) for i in range(2)]
        sums = jnp.sum(jnp.where(valid > 0.0, self.stat[0:6, :], 0.0), axis=1, keepdims=True)
        count = jnp.sum(valid, axis=1, keepdims=True)
        lane = lax.broadcasted_iota(jnp.int32, (6, D), 1)
        return jnp.concatenate(rows + [jnp.where(lane < 128, sums, count)], axis=0)


SCRATCH = dict(
    S=((2, D, T), F32), G=((D, T), F32), E=((D, T), F32), Y=((1024, T), F32),
    XA=((2, D, T), BF), XM=((2, D, T), BF), rhoA=((2, 8, T), F32), rhoM=((2, 8, T), F32),
    QA=((2, NQ, 128, T), BF), KT=((2, NK, H, T), BF), VT=((NK, H, T), BF),
    KTOK=((2, NK, T, 128), BF), VTOK=((2, NK, T, 128), BF), AT=((2, D, T), BF), M=((2, D, T), F32),
    GATE=((2, FF, T), BF), UP=((2, FF, T), BF), HID=((2, FF, T), BF),
    GLD=((OB * NF, T), BF), GLO=((1024, T), BF), DGU=((2 * FF, T), BF), DOA=((NQ, 128, T), BF),
    stat=((8, T), F32), valid=((8, T), F32), gacc=((2, D, 128), F32),
)
WEIGHTS = dict(WA=((D, 1024), BF), WO=((D, 1024), BF), WGU=((D, 2 * FF), BF), WDT=((OB * NF, FF), BF))
GRADS = dict(DA=((D, 1024), BF), DO=((D, 1024), BF), DG=((D, 2 * FF), BF), DD=((OB * NF, FF), BF))

def compute_kernel(order, names, *refs):
    w = Work(order, dict(zip(names, refs)))
    w.start()
    for r in range(2):
        w.project(r)
        w.attend(r)
        w.out_project(r)
        w.mlp(r)
    w.write_output()
    for r in (1, 0):
        w.mlp_back(r)
        w.attend_back(r)
        w.project_back(r)
    w.write_grad()
    w.tiny[...] = w.small()


def local_compute(order, x, length, ga, gm, ct, packed):
    cos, sin = rope_tables()
    ins = dict(length=length, x=x, ct=ct, ga=ga[:, None], gm=gm[:, None], cos=jnp.asarray(cos), sin=jnp.asarray(sin), **packed)
    outs = dict(out=((T, D), BF), gin=((T, D), F32), tiny=((8, D), F32), **GRADS)
    names = list(ins) + list(outs) + list(SCRATCH)
    vmem = pl.BlockSpec(memory_space=pltpu.VMEM)
    results = pl.pallas_call(
        functools.partial(compute_kernel, order, names),
        out_shape=[jax.ShapeDtypeStruct(*s) for s in outs.values()],
        in_specs=[pl.BlockSpec(memory_space=pltpu.SMEM)] + [vmem] * (len(ins) - 1),
        out_specs=[vmem] * len(outs),
        scratch_shapes=[pltpu.VMEM(*s) for s in SCRATCH.values()],
        compiler_params=pltpu.CompilerParams(vmem_limit_bytes=VMEM_LIMIT),
    )(*ins.values())
    return dict(zip(outs, results))


def pack(order, q, k, v, o, g, u, d):
    def cols(w, width):
        return w.reshape(w.shape[0], NF, width)[:, np.array(order)]
    zero = jnp.zeros((D, NF, 128 - QB - 2 * KB), BF)
    wa = jnp.concatenate([cols(q, QB), cols(k, KB), cols(v, KB), zero], axis=2).reshape(D, 1024)
    wo = jnp.pad(cols(o, QB), ((0, 0), (0, 0), (0, 128 - QB))).reshape(D, 1024)
    wgu = jnp.concatenate([cols(g, FB), cols(u, FB)], axis=2).reshape(D, 2 * FF)
    wd = jnp.pad(d.T.reshape(NF, QB, FF)[np.array(order)], ((0, 0), (0, OB - QB), (0, 0))).reshape(OB * NF, FF)
    return dict(WA=wa, WO=wo, WGU=wgu, WDT=wd)


def unpack(order, r):
    back = np.argsort(np.array(order))
    a = r["DA"].astype(F32).reshape(D, NF, 128)[:, back]
    o = r["DO"].astype(F32).reshape(D, NF, 128)[:, back, :QB].reshape(D, D)
    g = r["DG"].astype(F32).reshape(D, NF, 2 * FB)[:, back]
    d = r["DD"].astype(F32).reshape(NF, OB, FF)[back, :QB].reshape(D, FF).T
    return (
        a[:, :, :QB].reshape(D, D), a[:, :, QB : QB + KB].reshape(D, NK * H), a[:, :, QB + KB : QB + 2 * KB].reshape(D, NK * H),
        o, g[:, :, :FB].reshape(D, FF), g[:, :, FB:].reshape(D, FF), d,
    )


PIECES = ("A", "O", "G", "D")
WEIGHT_OF = dict(A="WA", O="WO", G="WGU", D="WDT")
GRAD_OF = dict(A="DA", O="DO", G="DG", D="DD")
WIDTH_OF = dict(A=128, O=128, G=2 * FB)
CUT_OF = dict(A=((0, 80), (80, 64)), O=((0, 64), (64, 80)), G=((0, 64), (64, 80)), D=((0, 256), (256, 128)))
ROWS = D // 4
LANES = FF // 4
MESH = pl.DeviceIdType.MESH


def region(ref, piece, dp, y, z, count, part=None):
    first, size = (0, None) if part is None else CUT_OF[piece][part]
    line = 4 * y + z
    if piece == "D":
        size = LANES if size is None else size
        rows = pl.ds(pl.multiple_of(OB * line, 16), OB * count)
        return ref.at[rows, pl.ds(pl.multiple_of(LANES * dp + first, 128), size)]
    size = ROWS if size is None else size
    width = WIDTH_OF[piece]
    rows = pl.ds(pl.multiple_of(ROWS * dp + first, 16), size)
    return ref.at[rows, pl.ds(pl.multiple_of(width * line, 128), width * count)]


def shape_of(piece, count, part=None):
    size = None if part is None else CUT_OF[piece][part][1]
    if piece == "D":
        return (OB * count, size or LANES)
    return (size or ROWS, WIDTH_OF[piece] * count)


class Links:
    def __init__(self, refs):
        self.__dict__.update(refs)
        self.dp, f = lax.axis_index("dp"), lax.axis_index("fsdp")
        self.x, self.c = self.dp // 2, lax.rem(self.dp, 2)
        self.z, self.y = f // 2, lax.rem(f, 2)
        self.far = 2 * (1 - self.x) + self.c
        self.other = 2 * self.x + 1 - self.c
        self.sib = (self.other, f)
        self.xn = (self.far, f)
        self.yn = (self.dp, 2 * self.z + 1 - self.y)
        self.peer = [None] + [lax.rem(self.z + k, 4) for k in (1, 2, 3)]
        self.zn = [None] + [(self.dp, 2 * self.peer[k] + self.y) for k in (1, 2, 3)]
        self.copies = {}
        self.used = 0

    def barrier(self):
        sem = pltpu.get_barrier_semaphore()
        partners = [self.sib, self.xn, self.yn] + self.zn[1:]
        for device in partners:
            pl.semaphore_signal(sem, inc=1, device_id=device, device_id_type=MESH)
        pl.semaphore_wait(sem, len(partners))

    def send(self, name, src, dst, device):
        copy = pltpu.make_async_remote_copy(
            src_ref=src,
            dst_ref=dst,
            send_sem=self.sent.at[self.used],
            recv_sem=self.came.at[self.used],
            device_id=device,
            device_id_type=MESH,
        )
        self.used += 1
        copy.start()
        self.copies[name] = copy

    def arrived(self, *names):
        for name in names:
            self.copies[name].wait_recv()

    def finish(self):
        for copy in self.copies.values():
            copy.wait_send()


    def own(self, p, y=None, z=0, count=4, part=None, dp=None):
        ref = getattr(self, WEIGHT_OF[p])
        return region(ref, p, self.dp if dp is None else dp, self.y if y is None else y, z, count, part)

    def spread(self, tag, p, part, device, dp=None, y=None, z=0, count=4):
        block = self.own(p, y, z, count, part, dp)
        self.send(("w", p, tag), block, block, device)

    def gather_start(self, p):
        for k in (1, 2, 3):
            self.spread(f"z{k}", p, None, self.zn[k], z=self.z, count=1)

    def gather_line(self, p):
        self.arrived(*[("w", p, f"z{k}") for k in (1, 2, 3)])
        self.spread("x", p, None, self.xn)
        self.spread("y", p, None, self.yn)
        self.spread("s", p, None, self.sib)

    def gather_cross(self, p):
        self.arrived(("w", p, "x"))
        self.spread("xy", p, 0, self.yn, dp=self.far)
        self.spread("sx", p, None, self.sib, dp=self.far)
        self.arrived(("w", p, "y"))
        self.spread("yx", p, 1, self.xn, y=1 - self.y)
        self.spread("sy", p, None, self.sib, y=1 - self.y)

    def gather_rest(self, p):
        self.arrived(("w", p, "xy"))
        self.spread("sxy", p, 0, self.sib, dp=self.far, y=1 - self.y)
        self.arrived(("w", p, "yx"))
        self.spread("syx", p, 1, self.sib, dp=self.far, y=1 - self.y)

    def gather_end(self, p):
        self.arrived(*[("w", p, tag) for tag in ("s", "sx", "sy", "sxy", "syx")])


    def term(self, p, dp, y, z=0, count=4, part=None):
        return region(getattr(self, GRAD_OF[p]), p, dp, y, z, count, part)

    def add(self, p, dp, y, part, came):
        at = self.term(p, dp, y, 0, 4, part)
        at[...] = at[...] + came[...]

    def sum_start(self, p):
        room = getattr(self, "one" + p)
        for i in range(2):
            for y in range(2):
                dp = 2 * i + 1 - self.c
                self.send(("g", p, "s", i, y), self.term(p, dp, y), room.at[i, y], self.sib)

    def sum_pair(self, p):
        room = getattr(self, "one" + p)
        for i in range(2):
            for y in range(2):
                self.arrived(("g", p, "s", i, y))
                self.add(p, 2 * i + self.c, y, None, room.at[i, y])
        ups, across = getattr(self, "twoy" + p), getattr(self, "twox" + p)
        for i, dp in enumerate((self.dp, self.far)):
            self.send(("g", p, "y", i), self.term(p, dp, 1 - self.y, part=0), ups.at[i], self.yn)
        for j, y in enumerate((self.y, 1 - self.y)):
            self.send(("g", p, "x", j), self.term(p, self.far, y, part=1), across.at[j], self.xn)

    def sum_cross(self, p):
        ups, across = getattr(self, "twoy" + p), getattr(self, "twox" + p)
        for i in (1, 0):
            self.arrived(("g", p, "y", i))
            self.add(p, (self.dp, self.far)[i], self.y, 0, ups.at[i])
            if i == 1:
                self.send(("g", p, "yx"), self.term(p, self.far, self.y, part=0), getattr(self, "threex" + p), self.xn)
        for j in (1, 0):
            self.arrived(("g", p, "x", j))
            self.add(p, self.dp, (self.y, 1 - self.y)[j], 1, across.at[j])
            if j == 1:
                self.send(("g", p, "xy"), self.term(p, self.dp, 1 - self.y, part=1), getattr(self, "threey" + p), self.yn)

    def sum_line(self, p):
        self.arrived(("g", p, "yx"))
        self.add(p, self.dp, self.y, 0, getattr(self, "threex" + p))
        self.arrived(("g", p, "xy"))
        self.add(p, self.dp, self.y, 1, getattr(self, "threey" + p))
        for k in (1, 2, 3):
            src = self.term(p, self.dp, self.y, self.peer[k], 1)
            self.send(("g", p, "z", k), src, getattr(self, "four" + p).at[k - 1], self.zn[k])

    def sum_end(self, p):
        total = self.term(p, self.dp, self.y, self.z, 1)[...].astype(F32)
        for k in (1, 2, 3):
            self.arrived(("g", p, "z", k))
            total = total + getattr(self, "four" + p)[k - 1].astype(F32)
        return total


    def tiny_step(self, step):
        if step > 0:
            self.arrived(("t", step - 1))
            self.tinies[step] = self.tinies[step - 1] + self.smallin[step - 1]
        if step < 3:
            self.send(("t", step), self.tinies.at[step], self.smallin.at[step], (self.sib, self.xn, self.yn)[step])
        else:
            for k in (1, 2, 3):
                self.send(("t", step, k), self.tinies.at[3], self.smallz.at[k], self.zn[k])

    def tiny_end(self):
        self.smallz[0] = self.tinies[3]
        for k in (1, 2, 3):
            self.arrived(("t", 3, k))
        total = None
        for z in range(4):
            k = lax.rem(self.z - z + 4, 4)
            term = self.smallz[k]
            total = term if total is None else total + term
        return total


def rooms():
    shapes = {}
    for p in PIECES:
        shapes["one" + p] = ((2, 2) + shape_of(p, 4), BF)
        shapes["twoy" + p] = ((2,) + shape_of(p, 4, 0), BF)
        shapes["twox" + p] = ((2,) + shape_of(p, 4, 1), BF)
        shapes["threex" + p] = (shape_of(p, 4, 0), BF)
        shapes["threey" + p] = (shape_of(p, 4, 1), BF)
        shapes["four" + p] = ((3,) + shape_of(p, 1), BF)
    shapes["tinies"] = ((4, 8, D), F32)
    shapes["smallin"] = ((3, 8, D), F32)
    shapes["smallz"] = ((4, 8, D), F32)
    return shapes


COPIES = 4 * 12 + 4 * 13 + 6


def pack_own(links, refs):
    rows = lambda *names: [refs[n][...].astype(F32) for n in names]
    zero = lambda n: jnp.zeros((ROWS, n), F32)
    links.own("A", z=links.z, count=1)[...] = jnp.concatenate(
        rows("q", "k", "v") + [zero(128 - QB - 2 * KB)], axis=1
    ).astype(BF)
    links.own("O", z=links.z, count=1)[...] = jnp.concatenate(rows("o") + [zero(128 - QB)], axis=1).astype(BF)
    links.own("G", z=links.z, count=1)[...] = jnp.concatenate(rows("g", "u"), axis=1).astype(BF)
    (down,) = rows("d")
    links.own("D", z=links.z, count=1)[...] = jnp.concatenate(
        [down.T, jnp.zeros((OB - QB, LANES), F32)], axis=0
    ).astype(BF)


def whole_kernel(order, names, *args):
    refs = dict(zip(names, args))
    w, links = Work(order, refs), Links(refs)
    links.barrier()
    pack_own(links, refs)
    for p in PIECES:
        links.gather_start(p)
    w.start()
    links.gather_line("A")
    links.gather_line("O")
    links.gather_cross("A")
    links.gather_line("G")
    links.gather_line("D")
    links.gather_cross("O")
    links.gather_rest("A")
    links.gather_end("A")
    w.project(0)
    links.gather_cross("G")
    links.gather_rest("O")
    w.attend(0)
    links.gather_end("O")
    w.out_project(0)
    links.gather_cross("D")
    links.gather_rest("G")
    links.gather_end("G")
    links.gather_rest("D")
    links.gather_end("D")
    w.mlp(0)
    w.project(1)
    w.attend(1)
    w.out_project(1)
    w.mlp(1)
    w.write_output()
    w.mlp_back(1)
    w.attend_back(1)
    w.project_back(1)
    w.mlp_back(0, links)
    w.attend_back(0, links)
    w.project_back(0, links)
    links.tinies[0] = w.small()
    links.tiny_step(0)
    links.sum_pair("A")
    links.sum_line("O")
    links.tiny_step(1)
    links.sum_cross("A")
    links.tiny_step(2)
    w.write_grad()
    total = links.sum_end("D")
    refs["gd"][...] = total[:QB, :].T
    total = links.sum_end("G")
    refs["gg"][...] = total[:, :FB]
    refs["gu"][...] = total[:, FB:]
    links.sum_line("A")
    links.tiny_step(3)
    total = links.sum_end("O")
    refs["go"][...] = total[:, :QB]
    total = links.sum_end("A")
    refs["gq"][...] = total[:, :QB]
    refs["gk"][...] = total[:, QB : QB + KB]
    refs["gv"][...] = total[:, QB + KB : QB + 2 * KB]
    total = links.tiny_end()
    refs["gga"][...] = total[0:1, :]
    refs["ggm"][...] = total[1:2, :]
    lane = lax.broadcasted_iota(jnp.int32, (1, 3), 1)
    for r in range(2):
        first, second, third = [total[2 + 3 * r + i : 3 + 3 * r + i, 0:3] for i in range(3)]
        sums = jnp.where(lane == 0, first, jnp.where(lane == 1, second, third))
        refs["rms"][r : r + 1, :] = jnp.sqrt(sums / (total[2:3, 128:131] * D))
    links.finish()


def whole(x, length, ga, q, k, v, o, gm, g, u, d, ct):
    order = [2 * (b % 4) + b // 4 for b in range(NF)]
    cos, sin = rope_tables()
    ins = dict(
        length=length, x=x[0], ct=ct[0], ga=ga[:, None], gm=gm[:, None], cos=jnp.asarray(cos), sin=jnp.asarray(sin),
        q=q, k=k, v=v, o=o, g=g, u=u, d=d,
    )
    outs = dict(
        out=((T, D), BF), gin=((T, D), F32), gga=((1, D), F32), gq=(q.shape, F32), gk=(k.shape, F32), gv=(v.shape, F32),
        go=(o.shape, F32), ggm=((1, D), F32), gg=(g.shape, F32), gu=(u.shape, F32), gd=(d.shape, F32), rms=((2, 3), F32),
    )
    scratch = dict(SCRATCH, **WEIGHTS, **GRADS, **rooms())
    names = list(ins) + list(outs) + list(scratch) + ["sent", "came"]
    vmem = pl.BlockSpec(memory_space=pltpu.VMEM)
    r = pl.pallas_call(
        functools.partial(whole_kernel, order, names),
        out_shape=[jax.ShapeDtypeStruct(*s) for s in outs.values()],
        in_specs=[pl.BlockSpec(memory_space=pltpu.SMEM)] + [vmem] * (len(ins) - 1),
        out_specs=[vmem] * len(outs),
        scratch_shapes=[pltpu.VMEM(*s) for s in scratch.values()]
        + [pltpu.SemaphoreType.DMA((COPIES,)), pltpu.SemaphoreType.DMA((COPIES,))],
        compiler_params=pltpu.CompilerParams(
            vmem_limit_bytes=VMEM_LIMIT, collective_id=0, has_side_effects=True
        ),
    )(*ins.values())
    r = dict(zip(outs, r))
    return (
        r["out"][None], r["gin"][None], r["gga"][0], r["gq"], r["gk"], r["gv"], r["go"], r["ggm"][0], r["gg"], r["gu"],
        r["gd"], r["rms"],
    )


def by_collectives(x, length, ga, q, k, v, o, gm, g, u, d, ct):
    order = list(range(NF))
    full = [lax.all_gather(lax.all_gather(w, "fsdp", axis=1, tiled=True), "dp", axis=0, tiled=True) for w in (q, k, v, o, g, u, d)]
    packed = pack(order, *full)
    results = [local_compute(order, x[i], length[i : i + 1], ga, gm, ct[i], packed) for i in range(x.shape[0])]
    out = jnp.stack([r["out"] for r in results])
    gin = jnp.stack([r["gin"] for r in results])
    tiny = lax.psum(sum(r["tiny"] for r in results), ("dp", "fsdp"))
    terms = [unpack(order, r) for r in results]
    grads = [
        lax.psum_scatter(
            lax.psum_scatter(sum(t), "dp", scatter_dimension=0, tiled=True), "fsdp", scatter_dimension=1, tiled=True
        )
        for t in zip(*terms)
    ]
    rms = jnp.sqrt(tiny[2:8, 0].reshape(2, 3) / (tiny[2, 128] * D))
    gq, gk, gv, go, gg, gu, gd = grads
    return out, gin, tiny[0], gq, gk, gv, go, tiny[1], gg, gu, gd, rms


def solution(mesh):
    blocks = P("dp", "fsdp")
    slots = P(("dp", "fsdp"), None, None)
    in_specs = (slots, P(("dp", "fsdp")), P(), blocks, blocks, blocks, blocks, P(), blocks, blocks, blocks, slots)
    out_specs = (slots, slots, P(), blocks, blocks, blocks, blocks, P(), blocks, blocks, blocks, P())

    def on_device(*args):
        fits = mesh.shape["dp"] == 4 and mesh.shape["fsdp"] == 8 and args[0].shape[0] == 1
        return (whole if fits else by_collectives)(*args)

    return jax.shard_map(on_device, mesh=mesh, in_specs=in_specs, out_specs=out_specs, check_vma=False)
```

time: 1080 us -> 183 us (0.17)
  waiting for transfers between devices: 552 us -> 0 us
  blocking collectives: 288 us -> 0 us
  Pallas kernels: 0 us -> 159 us
  matrix products: 157 us -> 0 us
  local copies, waits for them, and re-layouts: 46.9 us -> 21 us
  between operations: 17.3 us -> 1.43 us
    unnamed x24 -> x0, waiting for transfers between devices: 400 us -> none
    all_gather x11 -> x0, blocking collectives: 249 us -> none  [the longest x1 33.6 us: on_device(): lax.all_gather(gate_weight, 'fsdp', axis=1, tiled=True)]
    pallas_call x0 -> x1, Pallas kernels: none -> 159 us  [whole(): pl.pallas_call(functools.partial(whole_kernel, order, names), out_shape=[...]
    dot_general x54 -> x0, matrix products: 157 us -> none  [the longest x2 31.1 us: attend_backward(): jnp.einsum('ngqk,knd->qngd', grad_scores, heads_of_key, preferred_element...]
    reduce_scatter x7 -> x0, waiting for transfers between devices: 151 us -> none  [the longest x1 40.9 us: on_device(): lax.psum_scatter(total_down, 'dp', scatter_dimension=0, tiled=True)]
    psum x1 -> x0, blocking collectives: 39.7 us -> none  [on_device(): lax.psum((total_attn_gain, total_mlp_gain), ('dp', 'fsdp'))]
    unnamed x240 -> x37, local copies, waits for them, and re-layouts: 41 us -> 17.9 us
  transfers between devices with their start and end apart: 17 -> 0, of which waited for: 12 -> 0; matrix products, arithmetic and copies ran while one was open for 11% -> 0% of each run, Pallas kernels for 0% -> 0%
where the time goes in v1:
time: 183 us
  Pallas kernels  159 us (87%)
  local copies, waits for them, and re-layouts  21 us (11%)
    pallas_call x1, Pallas kernels, whole(): pl.pallas_call(functools.partial(whole_kernel, order, names), out_shape=[...  159 us
    unnamed x37, local copies, waits for them, and re-layouts  17.9 us

profile of v1, /device:TPU:0, one launch (start us, length us, event | category | flops | bytes accessed | tf_op | source)
XLA Modules:
  0.0 182.9 jit_solution(7841549257579693061)
XLA Ops:
  0.6 0.0 copy-start
  1.4 1.4 copy.40.args_8_
  2.8 1.4 copy.41.args_9_
  4.2 1.6 copy.42.args_13_
  5.8 1.5 broadcast_in_dim.16.args_3_
  7.3 1.5 broadcast_in_dim.17.args_4_
  8.9 2.1 %copy.36 = bf16[1,512,576]{2,1,0:T(8,128)(2,1)} copy(bf16[1,512,576]{1,2,0:T(8,128)(2,1)} %param.14) | data formatting | bytes 1179648 | tf_op args[0]
  11.0 0.0 copy-done
  11.0 1.1 copy.37
  12.1 159.3 %shard_map.229 = (bf16[512,576]{1,0:T(8,128)(2,1)}, f32[512,576]{1,0:T(8,128)}, f32[1,576]{1,0:T(1,128)}, f32[144,72]{1,0:T(8,128)}, f32[144,24]{1,0:T(8,128)}, ...) custom-call(s32[1]{0:T(128)S(6)} %copy.53.args_0_, ...), custom_call_target="tpu_custom_call" | custom-call | tf_op jit(solution)/shard_map/pallas_call | solution.py:749
  171.4 2.1 %copy.43 = bf16[1,512,576]{1,2,0:T(8,128)(2,1)} copy(bf16[1,512,576]{2,1,0:T(8,128)(2,1)} %bitcast.7) | data formatting | bytes 1179648
  173.5 0.0 copy-start.9
  173.5 0.0 copy-start.8
  173.5 0.0 copy-start.7
  173.5 0.0 copy-start.6
  173.5 0.0 copy-start.1
  173.5 0.0 copy-start.5
  173.5 0.0 copy-start.4
  173.6 0.0 copy-start.3
  173.6 0.0 copy-start.2
  173.6 2.8 %copy.44 = f32[1,512,576]{1,2,0:T(8,128)} copy(f32[1,512,576]{2,1,0:T(8,128)} %bitcast.6) | data formatting | bytes 2359296
  176.4 0.0 copy-done.9
  176.4 0.0 copy-start.10
  176.4 0.6 reduce
  177.0 0.0 copy-done.8
  177.0 0.6 reduce.1
  177.6 0.0 copy-done.7
  177.6 0.7 copy.45
  178.3 0.0 copy-done.6
  178.3 0.7 copy.46
  179.0 0.0 copy-done.1
  179.0 0.8 copy.47
  179.7 0.0 copy-done.5
  179.7 0.6 copy.54
  180.4 0.0 copy-done.4
  180.4 0.6 copy.55
  181.0 0.0 copy-done.3
  181.0 0.7 copy.56
  181.7 0.0 copy-done.2
  181.7 0.7 copy.57
  182.3 0.0 copy-done.10
  182.3 0.6 copy.58
Async XLA Ops:
  0.6 10.4 %copy-start = (bf16[1,512,576]{1,2,0:T(8,128)(2,1)S(1)}, bf16[1,512,576]{1,2,0:T(8,128)(2,1)}, u32[]{:S(2)}) copy-start(bf16[1,512,576]{1,2,0:T(8,128)(2,1)} %param.25) | copy-start | bytes 1769476
  173.5 2.9 %copy-start.9 = (f32[1,576]{1,0:T(1,128)S(1)}, f32[1,576]{1,0:T(1,128)}, u32[]{:S(2)}) copy-start(f32[1,576]{1,0:T(1,128)} %get-tuple-element.26) | copy-start | bytes 6916
  173.5 3.5 %copy-start.8 = (f32[1,576]{1,0:T(1,128)S(1)}, f32[1,576]{1,0:T(1,128)}, u32[]{:S(2)}) copy-start(f32[1,576]{1,0:T(1,128)} %get-tuple-element.31) | copy-start | bytes 6916
  173.5 4.1 %copy-start.7 = (f32[144,24]{1,0:T(8,128)S(1)}, f32[144,24]{1,0:T(8,128)}, u32[]{:S(2)}) copy-start(f32[144,24]{1,0:T(8,128)} %get-tuple-element.52) | copy-start | bytes 41476
  173.5 4.8 %copy-start.6 = (f32[144,24]{1,0:T(8,128)S(1)}, f32[144,24]{1,0:T(8,128)}, u32[]{:S(2)}) copy-start(f32[144,24]{1,0:T(8,128)} %get-tuple-element.53) | copy-start | bytes 41476
  173.5 5.4 %copy-start.1 = (f32[384,72]{1,0:T(8,128)S(1)}, f32[384,72]{1,0:T(8,128)}, u32[]{:S(2)}) copy-start(f32[384,72]{1,0:T(8,128)} %get-tuple-element.58) | copy-start | bytes 331780
  173.5 6.2 %copy-start.5 = (f32[144,72]{1,0:T(8,128)S(1)}, f32[144,72]{1,0:T(8,128)}, u32[]{:S(2)}) copy-start(f32[144,72]{1,0:T(8,128)} %get-tuple-element.75) | copy-start | bytes 124420
  173.5 6.8 %copy-start.4 = (f32[144,72]{1,0:T(8,128)S(1)}, f32[144,72]{1,0:T(8,128)}, u32[]{:S(2)}) copy-start(f32[144,72]{1,0:T(8,128)} %get-tuple-element.78) | copy-start | bytes 124420
  173.6 7.4 %copy-start.3 = (f32[144,192]{1,0:T(8,128)S(1)}, f32[144,192]{1,0:T(8,128)}, u32[]{:S(2)}) copy-start(f32[144,192]{1,0:T(8,128)} %get-tuple-element.80) | copy-start | bytes 331780
  173.6 8.1 %copy-start.2 = (f32[144,192]{1,0:T(8,128)S(1)}, f32[144,192]{1,0:T(8,128)}, u32[]{:S(2)}) copy-start(f32[144,192]{1,0:T(8,128)} %get-tuple-element.81) | copy-start | bytes 331780
  176.4 6.0 %copy-start.10 = (f32[2,3]{1,0:T(2,128)S(1)}, f32[2,3]{1,0:T(2,128)}, u32[]{:S(2)}) copy-start(f32[2,3]{1,0:T(2,128)} %get-tuple-element.83) | copy-start | bytes 76

commit v2 on v1

--- a/solution.py
+++ b/solution.py
@@ -26,6 +26,8 @@
 NEG = -1e30
 BLK = 256
 VMEM_LIMIT = 63 * 2**20
+ROWS = D // 4
+LANES = FF // 4
 BF = jnp.bfloat16
 F32 = jnp.float32
 
@@ -62,8 +64,10 @@
         valid = (place < count).astype(F32)
         self.valid[...] = valid
         for ts in lane_tiles():
-            self.S[0, :, ts] = self.x[ts, :].astype(F32).T
-            self.G[:, ts] = self.ct[ts, :].astype(F32).T * valid[0:1, ts]
+            self.S[0, :, ts] = self.x[:, ts].astype(F32)
+            self.G[:, ts] = jnp.where(valid[0:1, ts] > 0.0, self.ct[:, ts].astype(F32), 0.0)
+        self.gainA[...] = jnp.broadcast_to(self.ga[...], (128, D)).T
+        self.gainM[...] = jnp.broadcast_to(self.gm[...], (128, D)).T
         self.gacc[...] = jnp.zeros_like(self.gacc)
         self.QA[:, :, H:, :] = jnp.zeros((2, NQ, H, T), BF)
         self.DOA[:, H:, :] = jnp.zeros((NQ, H, T), BF)
@@ -89,8 +93,10 @@
             row += n
         return pieces[0] if len(pieces) == 1 else jnp.concatenate(pieces, axis=0)
 
+    def prepare(self, r):
+        self.norm(self.S, r, self.gainA, self.XA, self.rhoA, 3 * r)
+
     def project(self, r):
-        self.norm(self.S, r, self.ga, self.XA, self.rhoA, 3 * r)
         for c in range(2):
             cs = slice(512 * c, 512 * c + 512)
             self.Y[cs, :] = dot(self.WA[:, cs], self.XA[r], 0, 0)
@@ -132,7 +138,7 @@
         query = lax.broadcasted_iota(jnp.int32, (BLK, BLK), 1)
         return key <= query
 
-    def attend(self, r):
+    def attend(self, r, links=None):
         low, high = slice(0, BLK), slice(BLK, T)
 
         def head(h, carry):
@@ -162,7 +168,10 @@
             self.QA[r, h, H : H + 16, :] = jnp.concatenate(rows, axis=0).astype(BF)
             return carry
 
-        lax.fori_loop(0, NQ, head, 0)
+        for g in range(NK):
+            lax.fori_loop(GROUP * g, GROUP * g + GROUP, head, 0)
+            if links:
+                links.run(*HEADS[g])
 
     def out_project(self, r):
         for c in range(2):
@@ -178,8 +187,8 @@
                 squares = squares + y[8 * i : 8 * i + 8] * y[8 * i : 8 * i + 8]
         self.stat[3 * r + 1 : 3 * r + 2, :] = jnp.sum(squares, axis=0, keepdims=True)
 
-    def mlp(self, r):
-        self.norm(self.M, r, self.gm, self.XM, self.rhoM, None)
+    def mlp(self, r, links=None):
+        self.norm(self.M, r, self.gainM, self.XM, self.rhoM, None)
 
         def block(b, carry):
             f = 2 * lax.rem(b, 4) + b // 4 if self.order[1] == 2 else b
@@ -193,6 +202,8 @@
             return carry
 
         lax.fori_loop(0, NF, block, 0)
+        if links:
+            links.run(*BEFORE_DOWN)
         self.Y[0 : OB * NF, :] = dot(self.WDT[...], self.HID[r], 1, 0)
         squares = jnp.zeros((8, T), F32)
         for b in range(NF):
@@ -212,7 +223,7 @@
         valid = self.valid[0:1, :]
         for ts in lane_tiles():
             v = jnp.where(valid[:, ts] > 0.0, self.E[:, ts], 0.0)
-            self.out[ts, :] = v.T.astype(BF)
+            self.out[:, ts] = v.astype(BF)
 
     def pack_grad(self, dst, width):
         for b in range(NF):
@@ -240,7 +251,7 @@
             cs = slice(768 * c, 768 * c + 768)
             self.add_term(self.DD, (slice(None), cs), dot(self.GLD[...], self.HID[r, cs, :], 1, 1), r)
         if links:
-            links.sum_start("D")
+            links.run(*AFTER_DOWN)
 
         def block(z, carry):
             rows = pl.ds(pl.multiple_of(2 * FB * z, 128), 2 * FB)
@@ -261,10 +272,9 @@
             cs = slice(768 * c, 768 * c + 768)
             self.add_term(self.DG, (slice(None), cs), dot(self.XM[r], self.DGU[cs, :], 1, 1), r)
         if links:
-            links.sum_start("G")
-            links.sum_pair("D")
+            links.run(*AFTER_GATE)
         self.E[...] = dot(self.WGU[...], self.DGU[...], 1, 0)
-        self.norm_back(self.M, r, self.rhoM, self.gm, 1)
+        self.norm_back(self.M, r, self.rhoM, self.gainM, 1)
 
     def attend_back(self, r, links=None):
         self.pack_grad(self.GLO, 128)
@@ -272,9 +282,7 @@
             cs = slice(512 * c, 512 * c + 512)
             self.add_term(self.DO, (slice(None), cs), dot(self.AT[r], self.GLO[cs, :], 1, 1), r)
         if links:
-            links.sum_start("O")
-            links.sum_pair("G")
-            links.sum_cross("D")
+            links.run(*AFTER_OUT)
         self.E[...] = dot(self.WO[...], self.GLO[...], 1, 0)
         for h in range(NQ):
             rows = slice(H * h, H * h + H)
@@ -323,11 +331,8 @@
 
         for g in range(NK):
             lax.fori_loop(GROUP * g, GROUP * g + GROUP, head, 0)
-            if links and g == 0:
-                links.sum_pair("O")
-            if links and g == 1:
-                links.sum_cross("G")
-                links.sum_line("D")
+            if links:
+                links.run(*BACK_HEADS[g])
 
     def project_back(self, r, links=None):
         cos, sin = self.cos[...], self.sin[...]
@@ -352,15 +357,13 @@
             cs = slice(512 * c, 512 * c + 512)
             self.add_term(self.DA, (slice(None), cs), dot(self.XA[r], self.GLO[cs, :], 1, 1), r)
         if links:
-            links.sum_start("A")
-            links.sum_cross("O")
-            links.sum_line("G")
+            links.run(*AFTER_QKV)
         self.E[...] = dot(self.WA[...], self.GLO[...], 1, 0)
-        self.norm_back(self.S, r, self.rhoA, self.ga, 0)
+        self.norm_back(self.S, r, self.rhoA, self.gainA, 0)
 
     def write_grad(self):
         for ts in lane_tiles():
-            self.gin[ts, :] = self.G[:, ts].T
+            self.gin[:, ts] = self.G[:, ts]
 
     def small(self):
         valid = self.valid[0:1, :]
@@ -378,7 +381,7 @@
     KTOK=((2, NK, T, 128), BF), VTOK=((2, NK, T, 128), BF), AT=((2, D, T), BF), M=((2, D, T), F32),
     GATE=((2, FF, T), BF), UP=((2, FF, T), BF), HID=((2, FF, T), BF),
     GLD=((OB * NF, T), BF), GLO=((1024, T), BF), DGU=((2 * FF, T), BF), DOA=((NQ, 128, T), BF),
-    stat=((8, T), F32), valid=((8, T), F32), gacc=((2, D, 128), F32),
+    stat=((8, T), F32), valid=((8, T), F32), gacc=((2, D, 128), F32), gainA=((D, 128), F32), gainM=((D, 128), F32),
 )
 WEIGHTS = dict(WA=((D, 1024), BF), WO=((D, 1024), BF), WGU=((D, 2 * FF), BF), WDT=((OB * NF, FF), BF))
 GRADS = dict(DA=((D, 1024), BF), DO=((D, 1024), BF), DG=((D, 2 * FF), BF), DD=((OB * NF, FF), BF))
@@ -387,6 +390,7 @@
     w = Work(order, dict(zip(names, refs)))
     w.start()
     for r in range(2):
+        w.prepare(r)
         w.project(r)
         w.attend(r)
         w.out_project(r)
@@ -402,8 +406,8 @@
 
 def local_compute(order, x, length, ga, gm, ct, packed):
     cos, sin = rope_tables()
-    ins = dict(length=length, x=x, ct=ct, ga=ga[:, None], gm=gm[:, None], cos=jnp.asarray(cos), sin=jnp.asarray(sin), **packed)
-    outs = dict(out=((T, D), BF), gin=((T, D), F32), tiny=((8, D), F32), **GRADS)
+    ins = dict(length=length, x=x, ct=ct, ga=ga[None, :], gm=gm[None, :], cos=jnp.asarray(cos), sin=jnp.asarray(sin), **packed)
+    outs = dict(out=((D, T), BF), gin=((D, T), F32), tiny=((8, D), F32), **GRADS)
     names = list(ins) + list(outs) + list(SCRATCH)
     vmem = pl.BlockSpec(memory_space=pltpu.VMEM)
     results = pl.pallas_call(
@@ -440,39 +444,37 @@
     )
 
 
-PIECES = ("A", "O", "G", "D")
+PIECES = ("A", "O", "G0", "G1", "G2", "D0", "D1")
+CUT_OF = dict(
+    A=("A", 0, ROWS), O=("O", 0, ROWS), G0=("G", 0, 48), G1=("G", 48, 48), G2=("G", 96, 48), D0=("D", 0, 256), D1=("D", 256, 128)
+)
 WEIGHT_OF = dict(A="WA", O="WO", G="WGU", D="WDT")
 GRAD_OF = dict(A="DA", O="DO", G="DG", D="DD")
 WIDTH_OF = dict(A=128, O=128, G=2 * FB)
-CUT_OF = dict(A=((0, 80), (80, 64)), O=((0, 64), (64, 80)), G=((0, 64), (64, 80)), D=((0, 256), (256, 128)))
-ROWS = D // 4
-LANES = FF // 4
 MESH = pl.DeviceIdType.MESH
 
 
-def region(ref, piece, dp, y, z, count, part=None):
-    first, size = (0, None) if part is None else CUT_OF[piece][part]
-    line = 4 * y + z
-    if piece == "D":
-        size = LANES if size is None else size
+def region(refs, piece, dp, y, z, count):
+    matrix, first, size = CUT_OF[piece]
+    ref, line = refs[matrix], 4 * y + z
+    if matrix == "D":
         rows = pl.ds(pl.multiple_of(OB * line, 16), OB * count)
         return ref.at[rows, pl.ds(pl.multiple_of(LANES * dp + first, 128), size)]
-    size = ROWS if size is None else size
-    width = WIDTH_OF[piece]
+    width = WIDTH_OF[matrix]
     rows = pl.ds(pl.multiple_of(ROWS * dp + first, 16), size)
     return ref.at[rows, pl.ds(pl.multiple_of(width * line, 128), width * count)]
 
 
-def shape_of(piece, count, part=None):
-    size = None if part is None else CUT_OF[piece][part][1]
-    if piece == "D":
-        return (OB * count, size or LANES)
-    return (size or ROWS, WIDTH_OF[piece] * count)
+def shape_of(piece, count):
+    matrix, first, size = CUT_OF[piece]
+    return (OB * count, size) if matrix == "D" else (size, WIDTH_OF[matrix] * count)
 
 
 class Links:
     def __init__(self, refs):
         self.__dict__.update(refs)
+        self.weights = {m: refs[n] for m, n in WEIGHT_OF.items()}
+        self.grads = {m: refs[n] for m, n in GRAD_OF.items()}
         self.dp, f = lax.axis_index("dp"), lax.axis_index("fsdp")
         self.x, self.c = self.dp // 2, lax.rem(self.dp, 2)
         self.z, self.y = f // 2, lax.rem(f, 2)
@@ -514,151 +516,175 @@
         for copy in self.copies.values():
             copy.wait_send()
 
-
-    def own(self, p, y=None, z=0, count=4, part=None, dp=None):
-        ref = getattr(self, WEIGHT_OF[p])
-        return region(ref, p, self.dp if dp is None else dp, self.y if y is None else y, z, count, part)
-
-    def spread(self, tag, p, part, device, dp=None, y=None, z=0, count=4):
-        block = self.own(p, y, z, count, part, dp)
+    def run(self, *steps):
+        for step in steps:
+            kind, piece = step.split()
+            getattr(self, kind)(piece)
+
+
+    def spread(self, tag, p, device, dp=None, y=None, z=0, count=4):
+        block = region(self.weights, p, self.dp if dp is None else dp, self.y if y is None else y, z, count)
         self.send(("w", p, tag), block, block, device)
 
-    def gather_start(self, p):
-        for k in (1, 2, 3):
-            self.spread(f"z{k}", p, None, self.zn[k], z=self.z, count=1)
-
-    def gather_line(self, p):
+    def share(self, p):
+        for k in (1, 3, 2):
+            self.spread(f"z{k}", p, self.zn[k], z=self.z, count=1)
+
+    def line(self, p):
         self.arrived(*[("w", p, f"z{k}") for k in (1, 2, 3)])
-        self.spread("x", p, None, self.xn)
-        self.spread("y", p, None, self.yn)
-        self.spread("s", p, None, self.sib)
-
-    def gather_cross(self, p):
+        self.spread("x", p, self.xn)
+        self.spread("y", p, self.yn)
+        self.spread("s", p, self.sib)
+
+    def cross(self, p):
         self.arrived(("w", p, "x"))
-        self.spread("xy", p, 0, self.yn, dp=self.far)
-        self.spread("sx", p, None, self.sib, dp=self.far)
+        self.spread("xy", p, self.yn, dp=self.far, count=2)
+        self.spread("sx", p, self.sib, dp=self.far)
         self.arrived(("w", p, "y"))
-        self.spread("yx", p, 1, self.xn, y=1 - self.y)
-        self.spread("sy", p, None, self.sib, y=1 - self.y)
-
-    def gather_rest(self, p):
+        self.spread("yx", p, self.xn, y=1 - self.y, z=2, count=2)
+        self.spread("sy", p, self.sib, y=1 - self.y)
+
+    def rest(self, p):
         self.arrived(("w", p, "xy"))
-        self.spread("sxy", p, 0, self.sib, dp=self.far, y=1 - self.y)
+        self.spread("sxy", p, self.sib, dp=self.far, y=1 - self.y, count=2)
         self.arrived(("w", p, "yx"))
-        self.spread("syx", p, 1, self.sib, dp=self.far, y=1 - self.y)
-
-    def gather_end(self, p):
+        self.spread("syx", p, self.sib, dp=self.far, y=1 - self.y, z=2, count=2)
+
+    def end(self, p):
         self.arrived(*[("w", p, tag) for tag in ("s", "sx", "sy", "sxy", "syx")])
 
 
-    def term(self, p, dp, y, z=0, count=4, part=None):
-        return region(getattr(self, GRAD_OF[p]), p, dp, y, z, count, part)
-
-    def add(self, p, dp, y, part, came):
-        at = self.term(p, dp, y, 0, 4, part)
+    def term(self, p, dp, y, z=0, count=4):
+        return region(self.grads, p, dp, y, z, count)
+
+    def add(self, p, dp, y, z, count, came):
+        at = self.term(p, dp, y, z, count)
         at[...] = at[...] + came[...]
 
-    def sum_start(self, p):
+    def sibs(self, p):
         room = getattr(self, "one" + p)
         for i in range(2):
             for y in range(2):
                 dp = 2 * i + 1 - self.c
                 self.send(("g", p, "s", i, y), self.term(p, dp, y), room.at[i, y], self.sib)
 
-    def sum_pair(self, p):
+    def pair(self, p):
         room = getattr(self, "one" + p)
         for i in range(2):
             for y in range(2):
                 self.arrived(("g", p, "s", i, y))
-                self.add(p, 2 * i + self.c, y, None, room.at[i, y])
+                self.add(p, 2 * i + self.c, y, 0, 4, room.at[i, y])
         ups, across = getattr(self, "twoy" + p), getattr(self, "twox" + p)
         for i, dp in enumerate((self.dp, self.far)):
-            self.send(("g", p, "y", i), self.term(p, dp, 1 - self.y, part=0), ups.at[i], self.yn)
+            self.send(("g", p, "y", i), self.term(p, dp, 1 - self.y, 0, 2), ups.at[i], self.yn)
         for j, y in enumerate((self.y, 1 - self.y)):
-            self.send(("g", p, "x", j), self.term(p, self.far, y, part=1), across.at[j], self.xn)
-
-    def sum_cross(self, p):
+            self.send(("g", p, "x", j), self.term(p, self.far, y, 2, 2), across.at[j], self.xn)
+
+    def twos(self, p):
         ups, across = getattr(self, "twoy" + p), getattr(self, "twox" + p)
         for i in (1, 0):
             self.arrived(("g", p, "y", i))
-            self.add(p, (self.dp, self.far)[i], self.y, 0, ups.at[i])
+            self.add(p, (self.dp, self.far)[i], self.y, 0, 2, ups.at[i])
             if i == 1:
-                self.send(("g", p, "yx"), self.term(p, self.far, self.y, part=0), getattr(self, "threex" + p), self.xn)
+                self.send(("g", p, "yx"), self.term(p, self.far, self.y, 0, 2), getattr(self, "threex" + p), self.xn)
         for j in (1, 0):
             self.arrived(("g", p, "x", j))
-            self.add(p, self.dp, (self.y, 1 - self.y)[j], 1, across.at[j])
+            self.add(p, self.dp, (self.y, 1 - self.y)[j], 2, 2, across.at[j])
             if j == 1:
-                self.send(("g", p, "xy"), self.term(p, self.dp, 1 - self.y, part=1), getattr(self, "threey" + p), self.yn)
-
-    def sum_line(self, p):
+                self.send(("g", p, "xy"), self.term(p, self.dp, 1 - self.y, 2, 2), getattr(self, "threey" + p), self.yn)
+
+    def fours(self, p):
         self.arrived(("g", p, "yx"))
-        self.add(p, self.dp, self.y, 0, getattr(self, "threex" + p))
+        self.add(p, self.dp, self.y, 0, 2, getattr(self, "threex" + p))
         self.arrived(("g", p, "xy"))
-        self.add(p, self.dp, self.y, 1, getattr(self, "threey" + p))
-        for k in (1, 2, 3):
+        self.add(p, self.dp, self.y, 2, 2, getattr(self, "threey" + p))
+        for k in (1, 3, 2):
             src = self.term(p, self.dp, self.y, self.peer[k], 1)
             self.send(("g", p, "z", k), src, getattr(self, "four" + p).at[k - 1], self.zn[k])
 
-    def sum_end(self, p):
+    def total(self, p):
         total = self.term(p, self.dp, self.y, self.z, 1)[...].astype(F32)
         for k in (1, 2, 3):
             self.arrived(("g", p, "z", k))
             total = total + getattr(self, "four" + p)[k - 1].astype(F32)
-        return total
-
-
-    def tiny_step(self, step):
+        matrix, first, size = CUT_OF[p]
+        if matrix == "D":
+            self.sumD[:, first : first + size] = total[:QB, :]
+        else:
+            at = dict(A=0, O=128, G=256)[matrix]
+            self.sumN[first : first + size, at : at + WIDTH_OF[matrix]] = total
+
+
+    def tiny(self, step):
+        step = int(step)
         if step > 0:
             self.arrived(("t", step - 1))
-            self.tinies[step] = self.tinies[step - 1] + self.smallin[step - 1]
+            self.tinies[step] = self.tinies[step - 1] + self.tinyin[step - 1]
         if step < 3:
-            self.send(("t", step), self.tinies.at[step], self.smallin.at[step], (self.sib, self.xn, self.yn)[step])
+            self.send(("t", step), self.tinies.at[step], self.tinyin.at[step], (self.sib, self.xn, self.yn)[step])
         else:
             for k in (1, 2, 3):
-                self.send(("t", step, k), self.tinies.at[3], self.smallz.at[k], self.zn[k])
+                self.send(("t", step, k), self.tinies.at[3], self.tinyz.at[k], self.zn[k])
 
     def tiny_end(self):
-        self.smallz[0] = self.tinies[3]
+        self.tinyz[0] = self.tinies[3]
         for k in (1, 2, 3):
             self.arrived(("t", 3, k))
         total = None
         for z in range(4):
-            k = lax.rem(self.z - z + 4, 4)
-            term = self.smallz[k]
+            term = self.tinyz[lax.rem(self.z - z + 4, 4)]
             total = term if total is None else total + term
-        return total
+        self.sumT[...] = total
 
 
 def rooms():
     shapes = {}
     for p in PIECES:
         shapes["one" + p] = ((2, 2) + shape_of(p, 4), BF)
-        shapes["twoy" + p] = ((2,) + shape_of(p, 4, 0), BF)
-        shapes["twox" + p] = ((2,) + shape_of(p, 4, 1), BF)
-        shapes["threex" + p] = (shape_of(p, 4, 0), BF)
-        shapes["threey" + p] = (shape_of(p, 4, 1), BF)
+        for room in ("twoy", "twox"):
+            shapes[room + p] = ((2,) + shape_of(p, 2), BF)
+        for room in ("threex", "threey"):
+            shapes[room + p] = (shape_of(p, 2), BF)
         shapes["four" + p] = ((3,) + shape_of(p, 1), BF)
     shapes["tinies"] = ((4, 8, D), F32)
-    shapes["smallin"] = ((3, 8, D), F32)
-    shapes["smallz"] = ((4, 8, D), F32)
+    shapes["tinyin"] = ((3, 8, D), F32)
+    shapes["tinyz"] = ((4, 8, D), F32)
     return shapes
 
 
-COPIES = 4 * 12 + 4 * 13 + 6
+COPIES = len(PIECES) * (12 + 13) + 6
 
 
 def pack_own(links, refs):
     rows = lambda *names: [refs[n][...].astype(F32) for n in names]
     zero = lambda n: jnp.zeros((ROWS, n), F32)
-    links.own("A", z=links.z, count=1)[...] = jnp.concatenate(
-        rows("q", "k", "v") + [zero(128 - QB - 2 * KB)], axis=1
-    ).astype(BF)
-    links.own("O", z=links.z, count=1)[...] = jnp.concatenate(rows("o") + [zero(128 - QB)], axis=1).astype(BF)
-    links.own("G", z=links.z, count=1)[...] = jnp.concatenate(rows("g", "u"), axis=1).astype(BF)
-    (down,) = rows("d")
-    links.own("D", z=links.z, count=1)[...] = jnp.concatenate(
-        [down.T, jnp.zeros((OB - QB, LANES), F32)], axis=0
-    ).astype(BF)
+    q, k, v, o, g, u, d = rows("q", "k", "v", "o", "g", "u", "d")
+    whole = dict(
+        A=jnp.concatenate([q, k.T, v.T, zero(128 - QB - 2 * KB)], axis=1),
+        O=jnp.concatenate([o, zero(128 - QB)], axis=1),
+        G=jnp.concatenate([g, u], axis=1),
+        D=jnp.concatenate([d, jnp.zeros((OB - QB, LANES), F32)], axis=0),
+    )
+    for p in PIECES:
+        matrix, first, size = CUT_OF[p]
+        own = whole[matrix][:, first : first + size] if matrix == "D" else whole[matrix][first : first + size]
+        region(links.weights, p, links.dp, links.y, links.z, 1)[...] = own.astype(BF)
+
+
+BEGIN = ("share A", "share O", "share G0", "share G1", "share G2", "share D0", "share D1")
+BEFORE_PROJECT = ("line A", "line O", "cross A", "line G0", "cross O", "rest A", "line G1", "end A")
+AFTER_PROJECT = ("cross G0", "rest O", "line G2")
+HEADS = (("cross G1", "rest G0"), ("line D0",), ("cross G2", "rest G1"))
+BEFORE_OUT = ("end O", "line D1")
+BEFORE_MLP = ("cross D0", "rest G2", "end G0", "end G1", "end G2")
+BEFORE_DOWN = ("cross D1", "rest D0", "rest D1", "end D0", "end D1")
+AFTER_DOWN = ("sibs D0", "sibs D1")
+AFTER_GATE = ("sibs G0", "sibs G1", "sibs G2", "pair D0", "pair D1")
+AFTER_OUT = ("sibs O", "pair G0", "pair G1", "pair G2", "twos D0", "twos D1")
+BACK_HEADS = (("pair O", "fours D0"), ("twos G0", "fours D1"), ("twos G1", "fours G0"))
+AFTER_QKV = ("sibs A", "twos G2", "fours G1", "twos O", "fours G2")
+LAST = ("tiny 0", "pair A", "fours O", "tiny 1", "twos A", "tiny 2")
+VERY_LAST = ("total D0", "total D1", "total G0", "total G1", "total G2", "fours A", "tiny 3", "total O", "total A")
 
 
 def whole_kernel(order, names, *args):
@@ -666,29 +692,18 @@
     w, links = Work(order, refs), Links(refs)
     links.barrier()
     pack_own(links, refs)
-    for p in PIECES:
-        links.gather_start(p)
+    links.run(*BEGIN)
     w.start()
-    links.gather_line("A")
-    links.gather_line("O")
-    links.gather_cross("A")
-    links.gather_line("G")
-    links.gather_line("D")
-    links.gather_cross("O")
-    links.gather_rest("A")
-    links.gather_end("A")
+    w.prepare(0)
+    links.run(*BEFORE_PROJECT)
     w.project(0)
-    links.gather_cross("G")
-    links.gather_rest("O")
-    w.attend(0)
-    links.gather_end("O")
+    links.run(*AFTER_PROJECT)
+    w.attend(0, links)
+    links.run(*BEFORE_OUT)
     w.out_project(0)
-    links.gather_cross("D")
-    links.gather_rest("G")
-    links.gather_end("G")
-    links.gather_rest("D")
-    links.gather_end("D")
-    w.mlp(0)
+    links.run(*BEFORE_MLP)
+    w.mlp(0, links)
+    w.prepare(1)
     w.project(1)
     w.attend(1)
     w.out_project(1)
@@ -701,47 +716,42 @@
     w.attend_back(0, links)
     w.project_back(0, links)
     links.tinies[0] = w.small()
-    links.tiny_step(0)
-    links.sum_pair("A")
-    links.sum_line("O")
-    links.tiny_step(1)
-    links.sum_cross("A")
-    links.tiny_step(2)
+    links.run(*LAST)
     w.write_grad()
-    total = links.sum_end("D")
-    refs["gd"][...] = total[:QB, :].T
-    total = links.sum_end("G")
-    refs["gg"][...] = total[:, :FB]
-    refs["gu"][...] = total[:, FB:]
-    links.sum_line("A")
-    links.tiny_step(3)
-    total = links.sum_end("O")
-    refs["go"][...] = total[:, :QB]
-    total = links.sum_end("A")
-    refs["gq"][...] = total[:, :QB]
-    refs["gk"][...] = total[:, QB : QB + KB]
-    refs["gv"][...] = total[:, QB + KB : QB + 2 * KB]
-    total = links.tiny_end()
-    refs["gga"][...] = total[0:1, :]
-    refs["ggm"][...] = total[1:2, :]
+    links.run(*VERY_LAST)
+    links.tiny_end()
+    links.finish()
+
+
+def finish_kernel(*refs):
+    out, gin, sums, sumd, tiny, oout, ogin, ga, q, k, v, o, gm, g, u, d, rms = refs
+    oout[...] = out[...]
+    ogin[...] = gin[...]
+    q[...] = sums[:, :QB]
+    k[...] = sums[:, QB : QB + KB].T
+    v[...] = sums[:, QB + KB : QB + 2 * KB].T
+    o[...] = sums[:, 128 : 128 + QB]
+    g[...] = sums[:, 256 : 256 + FB]
+    u[...] = sums[:, 256 + FB : 256 + 2 * FB]
+    d[...] = sumd[...]
+    ga[...] = tiny[0:1, :]
+    gm[...] = tiny[1:2, :]
     lane = lax.broadcasted_iota(jnp.int32, (1, 3), 1)
     for r in range(2):
-        first, second, third = [total[2 + 3 * r + i : 3 + 3 * r + i, 0:3] for i in range(3)]
-        sums = jnp.where(lane == 0, first, jnp.where(lane == 1, second, third))
-        refs["rms"][r : r + 1, :] = jnp.sqrt(sums / (total[2:3, 128:131] * D))
-    links.finish()
+        first, second, third = [tiny[2 + 3 * r + i : 3 + 3 * r + i, 0:3] for i in range(3)]
+        squares = jnp.where(lane == 0, first, jnp.where(lane == 1, second, third))
+        rms[r : r + 1, :] = jnp.sqrt(squares / (tiny[2:3, 128:131] * D))
 
 
 def whole(x, length, ga, q, k, v, o, gm, g, u, d, ct):
     order = [2 * (b % 4) + b // 4 for b in range(NF)]
     cos, sin = rope_tables()
     ins = dict(
-        length=length, x=x[0], ct=ct[0], ga=ga[:, None], gm=gm[:, None], cos=jnp.asarray(cos), sin=jnp.asarray(sin),
-        q=q, k=k, v=v, o=o, g=g, u=u, d=d,
+        length=length, x=x[0].T, ct=ct[0].T, ga=ga[None, :], gm=gm[None, :], cos=jnp.asarray(cos), sin=jnp.asarray(sin),
+        q=q, k=k.T, v=v.T, o=o, g=g, u=u, d=d.T,
     )
     outs = dict(
-        out=((T, D), BF), gin=((T, D), F32), gga=((1, D), F32), gq=(q.shape, F32), gk=(k.shape, F32), gv=(v.shape, F32),
-        go=(o.shape, F32), ggm=((1, D), F32), gg=(g.shape, F32), gu=(u.shape, F32), gd=(d.shape, F32), rms=((2, 3), F32),
+        out=((D, T), BF), gin=((D, T), F32), sumN=((ROWS, 256 + 2 * FB), F32), sumD=((QB, LANES), F32), sumT=((8, D), F32)
     )
     scratch = dict(SCRATCH, **WEIGHTS, **GRADS, **rooms())
     names = list(ins) + list(outs) + list(scratch) + ["sent", "came"]
@@ -757,20 +767,26 @@
             vmem_limit_bytes=VMEM_LIMIT, collective_id=0, has_side_effects=True
         ),
     )(*ins.values())
-    r = dict(zip(outs, r))
-    return (
-        r["out"][None], r["gin"][None], r["gga"][0], r["gq"], r["gk"], r["gv"], r["go"], r["ggm"][0], r["gg"], r["gu"],
-        r["gd"], r["rms"],
-    )
+    rows = [
+        ((D, T), BF), ((D, T), F32), ((1, D), F32), (q.shape, F32), (k.shape[::-1], F32), (v.shape[::-1], F32),
+        (o.shape, F32), ((1, D), F32), (g.shape, F32), (u.shape, F32), (d.shape[::-1], F32), ((2, 3), F32),
+    ]
+    out, gin, ga, q, k, v, o, gm, g, u, d, rms = pl.pallas_call(
+        finish_kernel,
+        out_shape=[jax.ShapeDtypeStruct(*s) for s in rows],
+        in_specs=[vmem] * len(outs),
+        out_specs=[vmem] * len(rows),
+    )(*r)
+    return out.T[None], gin.T[None], ga[0], q, k.T, v.T, o, gm[0], g, u, d.T, rms
 
 
 def by_collectives(x, length, ga, q, k, v, o, gm, g, u, d, ct):
     order = list(range(NF))
     full = [lax.all_gather(lax.all_gather(w, "fsdp", axis=1, tiled=True), "dp", axis=0, tiled=True) for w in (q, k, v, o, g, u, d)]
     packed = pack(order, *full)
-    results = [local_compute(order, x[i], length[i : i + 1], ga, gm, ct[i], packed) for i in range(x.shape[0])]
-    out = jnp.stack([r["out"] for r in results])
-    gin = jnp.stack([r["gin"] for r in results])
+    results = [local_compute(order, x[i].T, length[i : i + 1], ga, gm, ct[i].T, packed) for i in range(x.shape[0])]
+    out = jnp.stack([r["out"].T for r in results])
+    gin = jnp.stack([r["gin"].T for r in results])
     tiny = lax.psum(sum(r["tiny"] for r in results), ("dp", "fsdp"))
     terms = [unpack(order, r) for r in results]
     grads = [

time: 183 us -> 155 us (0.85)
  local copies, waits for them, and re-layouts: 21 us -> 2.53 us
  Pallas kernels: 159 us -> 148 us
    unnamed x37 -> x0, local copies, waits for them, and re-layouts: 17.9 us -> none
    pallas_call x1, Pallas kernels: 159 us -> 145 us  [whole(): pl.pallas_call(functools.partial(whole_kernel, order, names), out_shape=[...]
    pallas_call x0 -> x1, Pallas kernels: none -> 3.31 us  [whole(): pl.pallas_call(finish_kernel, out_shape=[jax.ShapeDtypeStruct(*s) for s i...]
where the time goes in v2:
time: 155 us; the launch traced here: 154 us
  Pallas kernels  148 us (95%)
  other arithmetic  2.56 us (2%)
  local copies, waits for them, and re-layouts  2.53 us (2%)
    pallas_call x1, Pallas kernels, whole(): pl.pallas_call(functools.partial(whole_kernel, order, names), out_shape=[...  145 us
    pallas_call x1, Pallas kernels, whole(): pl.pallas_call(finish_kernel, out_shape=[jax.ShapeDtypeStruct(*s) for s i...  3.31 us

profile of v2, /device:TPU:0, one launch (start us, length us, event | category | flops | bytes accessed | tf_op | source)
XLA Modules:
  0.0 154.2 jit_solution(6148798060121815613)
XLA Ops:
  1.3 1.3 broadcast_in_dim.12.args_3_
  2.6 1.3 broadcast_in_dim.13.args_4_
  3.8 144.5 %shard_map.229 = (bf16[576,512]{1,0:T(8,128)(2,1)}, f32[576,512]{1,0:T(8,128)}, f32[144,640]{1,0:T(8,128)}, f32[72,384]{1,0:T(8,128)}, f32[8,576]{1,0:T(8,128)}) custom-call(s32[1]{0:T(128)S(6)} %copy.26.args_0_, bf16[576,512]{1,0:T(8,128)(2,1)} %bitcast.18, bf16[576,512]{1,0:T(8,128)(2,1)} %bitcast.19, f32[1,576]{1,0:T(1,128)} %broadcast_in_dim.12.args_3_, ...), custom_call_target="tpu_custom_call" | custom-call | tf_op jit(solution)/shard_map/pallas_call | solution.py:759
  148.4 3.3 %shard_map.230 = (bf16[576,512]{1,0:T(8,128)(2,1)}, f32[576,512]{1,0:T(8,128)}, f32[1,576]{1,0:T(1,128)}, f32[144,72]{1,0:T(8,128)}, f32[24,144]{1,0:T(8,128)}, ...) custom-call(bf16[576,512]{1,0:T(8,128)(2,1)} %get-tuple-element.29.r, ...), custom_call_target="tpu_custom_call" | custom-call | tf_op jit(solution)/shard_map/pallas_call | solution.py:774
  151.7 1.3 reduce
  153.0 1.3 reduce.1
